TPU v7x, 256 devices: a whole 4x4x8 slice. The times are simulated.
256 devices in a mesh: src: 32 (over z, x), tgt: 8 (over y, core).
Axes of the slice: x: 4, y: 4, z: 8, core: 2. Of those that a mesh axis runs over, the one named last changes fastest.
Arguments:
- sources: float32 [50, 16384], P(None, 'src'), may hold values from -1.2 to 1.2
- targets: float32 [50, 32768], P(None, 'tgt'), may hold values from -1.2 to 1.2
- pair_active: int32 [32, 8], P('src', 'tgt'), may hold values from 0 to 1, as said below
- count_src: int32 [32], replicated, may hold values from 256 to 512, as said below
- count_tgt: int32 [8], replicated, may hold values from 2048 to 4096, as said below
Outputs:
- source_potential: float32 [16384], P('src')
- target_potential: float32 [32768], P('tgt')
- ancestors: float32 [50, 32768], P(None, ('tgt', 'src'))
Inputs may be any that keep to these rules, and one draw needn't show every extreme that they name: `pair_active`: every source block has at least one listed tile and every target tile is listed with at least one source block. `count_src`: some block holds exactly 512 live cells and another exactly 256. `count_tgt`: some tile holds exactly 4096 live cells and another exactly 2048.
All inputs are finite; a program needn't handle non-finite values.
Results may differ from a plain program's by a relative error of at most 0.0003.
Values sent between devices are 32-bit elements; how exact they have to be, the bound alone decides.
A program may use at most 64 MiB of HBM per device.

v0:
```python
import jax
import jax.numpy as jnp
from jax import lax
from jax.sharding import PartitionSpec as P

ITERS = 4


EPS = 0.02
NEG = -1e30


def shards(sources, targets, pair_active, count_src, count_tgt):
    rows = sources.shape[1]
    cols = targets.shape[1]
    tiles_dev = pair_active.shape[1]
    tile = cols // tiles_dev
    src_index = lax.axis_index("src")
    tgt_index = lax.axis_index("tgt")
    log_a = -jnp.log(jnp.sum(count_src).astype(jnp.float32))
    log_b = -jnp.log(jnp.sum(count_tgt).astype(jnp.float32))
    row_live = jnp.arange(rows, dtype=jnp.int32) < count_src[src_index]
    tile_counts = lax.dynamic_slice_in_dim(count_tgt, tgt_index * tiles_dev, tiles_dev)
    within = jnp.arange(cols, dtype=jnp.int32) % tile
    col_live = within < jnp.repeat(tile_counts, tile)
    col_listed = col_live & jnp.repeat(pair_active[0] > 0, tile)
    allowed = row_live[:, None] & col_listed[None, :]
    left = jnp.sum(sources * sources, axis=0)
    right = jnp.sum(targets * targets, axis=0)
    cross = lax.dot_general(
        sources, targets, (((0,), (0,)), ((), ())), precision=lax.Precision.HIGHEST
    )
    cost = left[:, None] + right[None, :] - 2.0 * cross
    g = jnp.zeros((cols,), jnp.float32)
    f = jnp.zeros((rows,), jnp.float32)
    for step in range(ITERS):
        logits = jnp.where(allowed, (g[None, :] - cost) / EPS, NEG)
        peak = jnp.max(logits, axis=1)
        total = jnp.sum(jnp.where(allowed, jnp.exp(logits - peak[:, None]), 0.0), axis=1)
        best = lax.pmax(peak, "tgt")
        total = lax.psum(total * jnp.exp(peak - best), "tgt")
        peak = best
        f = jnp.where(
            row_live, EPS * (log_a - peak - jnp.log(jnp.where(row_live, total, 1.0))), 0.0
        )
        logits = jnp.where(allowed, (f[:, None] - cost) / EPS, NEG)
        peak = jnp.max(logits, axis=0)
        total = jnp.sum(jnp.where(allowed, jnp.exp(logits - peak[None, :]), 0.0), axis=0)
        best = lax.pmax(peak, "src")
        total = lax.psum(total * jnp.exp(peak - best), "src")
        peak = best
        g = jnp.where(
            col_live, EPS * (log_b - peak - jnp.log(jnp.where(col_live, total, 1.0))), 0.0
        )
    expo = jnp.where(allowed, (f[:, None] + g[None, :] - cost) / EPS - log_b, NEG)
    weight = jnp.where(allowed, jnp.exp(expo), 0.0)
    share = cols // lax.axis_size("src")
    whole = jnp.dot(sources, weight, precision=lax.Precision.HIGHEST)
    summed = lax.psum(whole, "src")
    ancestors = lax.dynamic_slice_in_dim(summed, src_index * share, share, 1)
    return (f, g, ancestors)


def solution(mesh):
    return jax.shard_map(
        shards,
        mesh=mesh,
        in_specs=(P(None, "src"), P(None, "tgt"), P("src", "tgt"), P(), P()),
        out_specs=(P("src"), P("tgt"), P(None, ("tgt", "src"))),
        check_vma=False,
    )
```

profile of v0, /device:TPU:1, one launch (start us, length us, event | category | flops | bytes accessed | tf_op | source)
XLA Modules:
  0.0 1479.2 jit_solution(10376923307877072454)
XLA Ops:
  17.1 12.3 fusion.14
  29.4 15.0 %pmax.56 = f32[512]{0:T(512)S(1)} all-reduce(f32[512]{0:T(512)S(1)} %get-tuple-element.3), channel_id=1, replica_groups=mesh['src'=32,'tgt'=8] {'tgt'}, use_global_device_ids=true, to_apply=%region_5.6 | all-reduce | flops 512 | bytes 4096 | tf_op jit(solution)/shard_map/pmax | solution.py:40
  49.6 13.1 psum.63
  67.9 5.3 fusion.1
  73.2 117.8 %pmax.57 = f32[4096]{0:T(1024)S(1)} all-reduce(f32[4096]{0:T(1024)S(1)} %fusion.15), channel_id=1, replica_groups=mesh['src'=32,'tgt'=8] {'src'}, use_global_device_ids=true, to_apply=%region_9.10 | all-reduce | flops 4096 | bytes 32768 | tf_op jit(solution)/shard_map/pmax | solution.py:49
  191.6 110.6 %psum.64 = f32[4096]{0:T(1024)S(1)} all-reduce(f32[4096]{0:T(1024)S(1)} %exponential_multiply_fusion.3), channel_id=1, replica_groups=mesh['src'=32,'tgt'=8] {'src'}, use_global_device_ids=true, to_apply=%region_11.12 | all-reduce | flops 4096 | bytes 32768 | tf_op jit(solution)/shard_map/psum | solution.py:50
  307.3 5.4 fusion.2
  312.8 67.6 %pmax.58 = f32[512]{0:T(512)S(1)} all-reduce(f32[512]{0:T(512)S(1)} %fusion.16), channel_id=1, replica_groups=mesh['src'=32,'tgt'=8] {'tgt'}, use_global_device_ids=true, to_apply=%region_13.14 | all-reduce | flops 512 | bytes 4096 | tf_op jit(solution)/shard_map/pmax | solution.py:40
  380.3 12.4 psum.65
  403.2 109.9 %pmax.59 = f32[4096]{0:T(1024)S(1)} all-reduce(f32[4096]{0:T(1024)S(1)} %fusion.17), channel_id=1, replica_groups=mesh['src'=32,'tgt'=8] {'src'}, use_global_device_ids=true, to_apply=%region_17.18 | all-reduce | flops 4096 | bytes 32768 | tf_op jit(solution)/shard_map/pmax | solution.py:49
  513.1 110.3 %psum.66 = f32[4096]{0:T(1024)S(1)} all-reduce(f32[4096]{0:T(1024)S(1)} %exponential_multiply_fusion.2), channel_id=1, replica_groups=mesh['src'=32,'tgt'=8] {'src'}, use_global_device_ids=true, to_apply=%region_19.20 | all-reduce | flops 4096 | bytes 32768 | tf_op jit(solution)/shard_map/psum | solution.py:50
  628.5 5.4 fusion.4
  633.9 67.6 %pmax.60 = f32[512]{0:T(512)S(1)} all-reduce(f32[512]{0:T(512)S(1)} %fusion.18), channel_id=1, replica_groups=mesh['src'=32,'tgt'=8] {'tgt'}, use_global_device_ids=true, to_apply=%region_21.22 | all-reduce | flops 512 | bytes 4096 | tf_op jit(solution)/shard_map/pmax | solution.py:40
  701.5 12.6 psum.67
  719.2 5.3 fusion.5
  724.5 109.9 %pmax.61 = f32[4096]{0:T(1024)S(1)} all-reduce(f32[4096]{0:T(1024)S(1)} %fusion.19), channel_id=1, replica_groups=mesh['src'=32,'tgt'=8] {'src'}, use_global_device_ids=true, to_apply=%region_25.26 | all-reduce | flops 4096 | bytes 32768 | tf_op jit(solution)/shard_map/pmax | solution.py:49
  834.4 110.3 %psum.68 = f32[4096]{0:T(1024)S(1)} all-reduce(f32[4096]{0:T(1024)S(1)} %exponential_multiply_fusion.1), channel_id=1, replica_groups=mesh['src'=32,'tgt'=8] {'src'}, use_global_device_ids=true, to_apply=%region_27.28 | all-reduce | flops 4096 | bytes 32768 | tf_op jit(solution)/shard_map/psum | solution.py:50
  949.9 5.4 fusion.6
  955.3 67.6 %pmax.62 = f32[512]{0:T(512)S(1)} all-reduce(f32[512]{0:T(512)S(1)} %fusion.20), channel_id=1, replica_groups=mesh['src'=32,'tgt'=8] {'tgt'}, use_global_device_ids=true, to_apply=%region_29.30 | all-reduce | flops 512 | bytes 4096 | tf_op jit(solution)/shard_map/pmax | solution.py:40
  1022.9 12.4 psum.69
  1040.5 109.9 %pmax.63 = f32[4096]{0:T(1024)S(1)} all-reduce(f32[4096]{0:T(1024)S(1)} %fusion.21), channel_id=1, replica_groups=mesh['src'=32,'tgt'=8] {'src'}, use_global_device_ids=true, to_apply=%region_33.34 | all-reduce | flops 4096 | bytes 32768 | tf_op jit(solution)/shard_map/pmax | solution.py:49
  1155.6 110.6 %psum.70 = f32[4096]{0:T(1024)S(1)} all-reduce(f32[4096]{0:T(1024)S(1)} %exponential_multiply_fusion), channel_id=1, replica_groups=mesh['src'=32,'tgt'=8] {'src'}, use_global_device_ids=true, to_apply=%region_35.36 | all-reduce | flops 4096 | bytes 32768 | tf_op jit(solution)/shard_map/psum | solution.py:50
  1266.9 11.6 fusion.22
  1278.6 192.5 %all-reduce.2.cloned.1.call-done = f32[50,4096]{1,0:T(8,128)} async-done(((f32[50,4096]{1,0:T(8,128)}), f32[50,4096]{1,0:T(8,128)}) %all-reduce.2.cloned.1.call-update) | async-done | bytes 819216 | tf_op jit(solution)/shard_map/psum | solution.py:59
  (43 shorter events, 62.4 us)
Async XLA Ops:
  7.2 1463.9 %all-reduce.2.cloned.1.call-start = ((), (), s32[]{:S(2)}) async-start(), calls=%async_computation | async-start | bytes 1835008 | tf_op jit(solution)/shard_map/psum | solution.py:59
  1036.0 230.9 %copy-start.1 = (f32[512]{0:T(512)}, f32[512]{0:T(512)S(1)}, u32[]{:S(2)}) copy-start(f32[512]{0:T(512)S(1)} %multiply_select_fusion.4) | copy-start | bytes 6148
  1036.0 230.9 %copy-start = (f32[50,512]{1,0:T(8,128)S(1)}, f32[50,512]{1,0:T(8,128)}, u32[]{:S(2)}) copy-start(f32[50,512]{1,0:T(8,128)} %param.5) | copy-start | bytes 307204
  1266.9 11.7 copy-start.2
Sparse Core Ops, SparseCore 0:
  1278.7 192.3 all-reduce.1
where the time goes:
time: 1480 us
  blocking collectives  1160 us (78%)
  waiting for transfers between devices  192 us (13%)
  other arithmetic  85.2 us (6%)
  matrix products  23.9 us (2%)
  between operations  16.2 us (1%)
    pmax x4, blocking collectives, shards(): best = lax.pmax(peak, 'src')  447 us
    psum x4, blocking collectives, shards(): total = lax.psum(total * jnp.exp(peak - best), 'src')  442 us
    pmax x4, blocking collectives, shards(): best = lax.pmax(peak, 'tgt')  218 us
    psum x1, waiting for transfers between devices, shards(): summed = lax.psum(whole, 'src')  192 us
    psum x4, blocking collectives, shards(): total = lax.psum(total * jnp.exp(peak - best), 'tgt')  50.6 us
  transfers between devices with their start and end apart: 1, of which 1 were waited for; matrix products, arithmetic and copies ran while one was open for 0% of the time, Pallas kernels for 0%

commit v1 on v0

v1 whole, which is shorter than its diff:
```python
import functools
import math

import jax
import jax.numpy as jnp
from jax import lax
from jax.experimental import pallas as pl
from jax.experimental.pallas import tpu as pltpu
from jax.sharding import PartitionSpec as P

ITERS = 4
EPS = 0.02
SCALE = math.log2(math.e) / EPS
NEG = -(2.0**100)
LOW = -3.0e38
MESH = pl.DeviceIdType.MESH

DIMS = 50
PAD = 64
ROWS = 1024
COLS = 2048
LANES = 128
ROW_BLOCKS = ROWS // LANES
COL_BLOCKS = COLS // LANES
X_CHIPS = 4
Y_CHIPS = 4
Z_CHIPS = 8
CORES = 2

OVER_XY = sorted(
    [(0, dx, dy, 0) for dx in range(X_CHIPS) for dy in range(Y_CHIPS) if dx or dy],
    key=lambda d: -(min(d[1], X_CHIPS - d[1]) + min(d[2], Y_CHIPS - d[2])),
)
OVER_Z_CORE = sorted(
    [(dz, 0, 0, dc) for dz in range(Z_CHIPS) for dc in range(CORES) if dz or dc],
    key=lambda d: -min(d[0], Z_CHIPS - d[0]),
)
OVER_X_CORE = [(0, dx, 0, dc) for dx in range(X_CHIPS) for dc in range(CORES) if dx or dc]
OVER_X = [(0, 2, 0, 0), (0, 1, 0, 0), (0, 3, 0, 0)]
OTHER_CORE = (0, 0, 0, 1)
PARTNERS = OVER_XY + OVER_Z_CORE + [d for d in OVER_X_CORE if d[1] and d[3]]


def tree(op, parts):
    while len(parts) > 1:
        parts = [op(*parts[i : i + 2]) if i + 1 < len(parts) else parts[i] for i in range(0, len(parts), 2)]
    return parts[0]


def log_sum(parts):
    peak = tree(jnp.maximum, parts)
    total = tree(jnp.add, [jnp.exp2(p - peak) for p in parts])
    return peak + jnp.log2(total)


def split(value, pieces):
    out = []
    for _ in range(pieces):
        piece = value.astype(jnp.bfloat16)
        out.append(piece)
        value = value - piece.astype(jnp.float32)
    return out


def kernel(
    count_src, count_tgt, pair, src, tgt,
    f_out, g_out, anc_out,
    flags, x_in, y_in, x_full, y_full, x_stack, x_lines, y_stack, x_pieces,
    logits, row_peak, row_total, f_rep, g_rep, col_peak, col_total,
    row_box, col_box, f_box, g_box, num_box,
    flag_sems, x_send, x_recv, y_sems, row_send, row_recv, col_send, col_recv, f_sems, g_sems, num_sems,
):
    at_src = lax.axis_index("src")
    at_tgt = lax.axis_index("tgt")
    z, x = at_src // X_CHIPS, lax.rem(at_src, X_CHIPS)
    y, c = at_tgt // CORES, lax.rem(at_tgt, CORES)
    half = x // 2

    def device(d):
        dz, dx, dy, dc = d
        return (
            lax.rem(z + dz, Z_CHIPS) * X_CHIPS + lax.rem(x + dx, X_CHIPS),
            lax.rem(y + dy, Y_CHIPS) * CORES + lax.rem(c + dc, CORES),
        )

    def remote(a, b, send, recv, d):
        return pltpu.make_async_remote_copy(
            src_ref=a, dst_ref=b, send_sem=send, recv_sem=recv, device_id=device(d), device_id_type=MESH
        )

    barrier = pltpu.get_barrier_semaphore()
    for d in PARTNERS:
        pl.semaphore_signal(barrier, inc=1, device_id=device(d), device_id_type=MESH)

    mine = x * CORES + c
    listed = (pair[0, 0] > 0).astype(jnp.float32)
    flags[mine] = jnp.full((1, LANES), listed, jnp.float32)
    for k in range(Z_CHIPS):
        at = pl.multiple_of((k * X_CHIPS + x) * LANES, LANES)
        y_in[c, :, k * LANES : (k + 1) * LANES] = tgt[:, pl.ds(at, LANES)]

    pl.semaphore_wait(barrier, len(PARTNERS))

    y_copy = remote(y_in.at[c], y_in.at[c], y_sems.at[0], y_sems.at[1], OTHER_CORE)
    y_copy.start()
    x_copies = [remote(src, x_in.at[lax.rem(x, 2)], x_send, x_recv.at[lax.rem(x, 2)], d) for d in OVER_X]

    @pl.when(half == c)
    def _():
        for copy in x_copies:
            copy.start()
        x_in[lax.rem(x, 2)] = src[...]

    flag_copies = [remote(flags.at[mine], flags.at[mine], flag_sems.at[0], flag_sems.at[1], d) for d in OVER_X_CORE]
    for copy in flag_copies:
        copy.start()

    def number_of(counts, length):
        total = counts[0]
        for i in range(1, length):
            total = total + counts[i]
        return total.astype(jnp.float32)

    log_a = -jnp.log2(jnp.full((8, LANES), number_of(count_src, Z_CHIPS * X_CHIPS), jnp.float32))
    log_b = -jnp.log2(jnp.full((COL_BLOCKS, LANES), number_of(count_tgt, Y_CHIPS * CORES), jnp.float32))
    row_counts = [count_src[z * X_CHIPS + 2 * c + i] for i in range(2)]
    col_counts = [count_tgt[y * CORES + i] for i in range(CORES)]

    def row_ok(block, lane):
        within = lax.rem(block, 4) * LANES + lane
        return within < jnp.where(block < 4, row_counts[0], row_counts[1])

    def col_ok(block, lane):
        within = (lax.rem(block, Z_CHIPS) * X_CHIPS + x) * LANES + lane
        return within < jnp.where(block < Z_CHIPS, col_counts[0], col_counts[1])

    def places(shape):
        return lax.broadcasted_iota(jnp.int32, shape, 0), lax.broadcasted_iota(jnp.int32, shape, 1)

    row_live = row_ok(*places((ROW_BLOCKS, LANES)))
    col_live = col_ok(*places((COL_BLOCKS, LANES)))
    along_rows = lax.broadcasted_iota(jnp.int32, (1, ROWS), 1)
    along_cols = lax.broadcasted_iota(jnp.int32, (1, COLS), 1)
    dead_rows = jnp.where(row_ok(along_rows // LANES, lax.rem(along_rows, LANES)), 0.0, NEG)
    dead_cols = jnp.where(col_ok(along_cols // LANES, lax.rem(along_cols, LANES)), 0.0, NEG)

    def flags_received():
        d = remote(flags.at[pl.ds(0, len(OVER_X_CORE))], flags.at[pl.ds(0, len(OVER_X_CORE))], flag_sems.at[0], flag_sems.at[1], OTHER_CORE)
        d.wait_recv()
        d.wait_send()

    flags_received()

    @pl.when(x != 2 * c)
    def _():
        remote(x_in.at[0], x_in.at[0], x_send, x_recv.at[0], OVER_X[0]).wait_recv()

    @pl.when(x != 2 * c + 1)
    def _():
        remote(x_in.at[1], x_in.at[1], x_send, x_recv.at[1], OVER_X[0]).wait_recv()

    x_full[DIMS:PAD, :] = jnp.zeros((PAD - DIMS, ROWS), jnp.float32)
    for i in range(2):
        x_full[0:DIMS, i * 512 : (i + 1) * 512] = x_in[i]
    first, second = split(x_full[...], 2)
    x_pieces[0:PAD, :] = first
    x_pieces[PAD:, :] = second
    x_full[0:DIMS, :] = x_full[0:DIMS, :] * (2.0 * SCALE)
    x_full[DIMS : DIMS + 1, :] = jnp.where(along_rows < 512, 1.0, 0.0)
    x_full[DIMS + 1 : DIMS + 2, :] = jnp.where(along_rows < 512, 0.0, 1.0)
    x_full[DIMS + 2 : DIMS + 3, :] = dead_rows
    p1, p2, p3 = split(x_full[...], 3)
    for i, p in enumerate((p1, p1, p2, p1, p3, p2)):
        x_stack[i * PAD : (i + 1) * PAD, :] = p
    for i in range(ROW_BLOCKS):
        x_lines[i * LANES : (i + 1) * LANES, :] = x_stack[:, i * LANES : (i + 1) * LANES].T

    y_copy.wait_recv()
    y_full[DIMS:PAD, :] = jnp.zeros((PAD - DIMS, COLS), jnp.float32)
    for i in range(CORES):
        at = pl.ds(i * (COLS // 2), COLS // 2)
        y_full[0:DIMS, at] = y_in[i]
        for k in range(2):
            unlisted = jnp.where(flags[(2 * c + k) * CORES + i] > 0, 0.0, NEG)
            y_full[DIMS + k : DIMS + k + 1, at] = jnp.concatenate([unlisted] * Z_CHIPS, axis=1)
    y_full[DIMS : DIMS + 1, :] = jnp.minimum(y_full[DIMS : DIMS + 1, :], dead_cols)
    y_full[DIMS + 1 : DIMS + 2, :] = jnp.minimum(y_full[DIMS + 1 : DIMS + 2, :], dead_cols)
    y_full[DIMS + 2 : DIMS + 3, :] = jnp.ones((1, COLS), jnp.float32)
    for b in range(COL_BLOCKS):
        block = y_full[0:DIMS, b * LANES : (b + 1) * LANES]
        first_g = -SCALE * jnp.sum(block * block, axis=0, keepdims=True)
        g_rep[b] = jnp.broadcast_to(first_g, (8, LANES))
        p1, p2, p3 = split(y_full[:, b * LANES : (b + 1) * LANES], 3)
        for i, p in enumerate((p1, p2, p1, p3, p1, p2)):
            y_stack[i * PAD : (i + 1) * PAD, b * LANES : (b + 1) * LANES] = p

    def logits_of(k, _):
        at = pl.ds(pl.multiple_of(k * 256, 256), 256)
        logits[:, at] = jnp.dot(x_lines[...], y_stack[:, at], preferred_element_type=jnp.float32)
        return 0

    lax.fori_loop(0, COLS // 256, logits_of, 0)

    def row_step(it):
        g = [g_rep[b] for b in range(COL_BLOCKS)]

        def body(k, _):
            at = pl.ds(pl.multiple_of(k * 8, 8), 8)
            parts = [logits[at, b * LANES : (b + 1) * LANES] + g[b] for b in range(COL_BLOCKS)]
            peak = tree(jnp.maximum, parts)
            row_peak[at, :] = peak
            row_total[at, :] = tree(jnp.add, [jnp.exp2(p - peak) for p in parts])
            return 0

        lax.fori_loop(0, ROWS // 8, body, 0, unroll=4)
        own = row_box.at[it, len(OVER_XY)]
        for b in range(ROW_BLOCKS):
            peaks = row_peak[b * LANES : (b + 1) * LANES, :].T
            totals = row_total[b * LANES : (b + 1) * LANES, :].T
            peak = jnp.max(peaks, axis=0, keepdims=True)
            total = jnp.sum(totals * jnp.exp2(peaks - peak), axis=0, keepdims=True)
            own[b : b + 1, :] = peak + jnp.log2(total)
        for r, d in enumerate(OVER_XY):
            remote(own, row_box.at[it, r], row_send.at[it], row_recv.at[it], d).start()
        row_all(it).wait_recv()
        total = log_sum([row_box[it, r] for r in range(len(OVER_XY) + 1)])
        f = jnp.where(row_live, log_a - total, 0.0)
        for b in range(ROW_BLOCKS):
            f_rep[b * LANES : (b + 1) * LANES, :] = jnp.broadcast_to(f[b : b + 1, :], (LANES, LANES)).T
        return f

    def row_all(it):
        some = row_box.at[it, pl.ds(0, len(OVER_XY))]
        return remote(some, some, row_send.at[it], row_recv.at[it], OVER_XY[0])

    def col_start(it):
        def pair_of_blocks(q, _):
            cols = [pl.ds(pl.multiple_of((2 * q + i) * LANES, LANES), LANES) for i in range(2)]

            def body(k, carry):
                base = pl.multiple_of(k * 64, 64)
                f = [f_rep[pl.ds(base + 8 * j, 8), :] for j in range(8)]
                out = []
                for i in range(2):
                    peak, total = carry[2 * i : 2 * i + 2]
                    parts = [logits[pl.ds(base + 8 * j, 8), cols[i]] + f[j] for j in range(8)]
                    best = jnp.maximum(peak, tree(jnp.maximum, parts))
                    fresh = tree(jnp.add, [jnp.exp2(p - best) for p in parts])
                    out += [best, total * jnp.exp2(peak - best) + fresh]
                return tuple(out)

            low, zero = jnp.full((8, LANES), LOW, jnp.float32), jnp.zeros((8, LANES), jnp.float32)
            done = lax.fori_loop(0, ROWS // 64, body, (low, zero, low, zero), unroll=4)
            for i in range(2):
                col_peak[2 * q + i] = done[2 * i]
                col_total[2 * q + i] = done[2 * i + 1]
            return 0

        lax.fori_loop(0, COL_BLOCKS // 2, pair_of_blocks, 0)
        own = col_box.at[it, len(OVER_Z_CORE)]
        peaks = col_peak[...]
        peak = jnp.max(peaks, axis=1, keepdims=True)
        total = jnp.sum(col_total[...] * jnp.exp2(peaks - peak), axis=1)
        own[...] = peak[:, 0, :] + jnp.log2(total)
        for r, d in enumerate(OVER_Z_CORE):
            remote(own, col_box.at[it, r], col_send.at[it], col_recv.at[it], d).start()

    def col_all(it):
        some = col_box.at[it, pl.ds(0, len(OVER_Z_CORE))]
        return remote(some, some, col_send.at[it], col_recv.at[it], OVER_Z_CORE[0])

    def col_end(it):
        col_all(it).wait_recv()
        total = log_sum([col_box[it, r] for r in range(len(OVER_Z_CORE) + 1)])
        return jnp.where(col_live, log_b - total, 0.0)

    def iteration(it, _):
        row_step(it)
        col_start(it)
        g = col_end(it)
        for b in range(COL_BLOCKS):
            g_rep[b] = jnp.broadcast_to(g[b : b + 1, :], (8, LANES))
        return 0

    lax.fori_loop(0, ITERS - 1, iteration, 0)
    last = ITERS - 1
    f_box[0] = row_step(last)
    f_copy = remote(f_box.at[0], f_box.at[1], f_sems.at[0], f_sems.at[1], OTHER_CORE)
    f_copy.start()
    col_start(last)

    for b in range(COL_BLOCKS):
        col_peak[b] = jnp.broadcast_to(col_box[last, len(OVER_Z_CORE), b : b + 1, :], (8, LANES))

    def ancestors_of(k, _):
        step = (k + 1) // 2
        dz = jnp.where(lax.rem(k, 2) == 0, 4 + step, 4 - step)
        to = lax.rem(z + dz, Z_CHIPS)
        cols = [pl.ds(pl.multiple_of((i * Z_CHIPS + to) * LANES, LANES), LANES) for i in range(CORES)]
        local = [col_peak[i * Z_CHIPS + to] for i in range(CORES)]
        acc = jnp.zeros((PAD, CORES * LANES), jnp.float32)
        for r in range(ROWS // 256):
            at = slice(r * 256, (r + 1) * 256)
            f = f_rep[at, :]
            weight = jnp.concatenate(
                [jnp.exp2(logits[at, cols[i]] + (f - local[i][0:1, :])) for i in range(CORES)], axis=1
            )
            w1, w2 = split(weight, 2)
            both = jnp.dot(x_pieces[:, at], w1, preferred_element_type=jnp.float32)
            acc += both[0:PAD] + both[PAD:] + jnp.dot(x_pieces[0:PAD, at], w2, preferred_element_type=jnp.float32)
        for i in range(CORES):
            dc = lax.rem(i + c, CORES)
            slot = dc * Z_CHIPS + dz
            num_box[0, slot] = acc[0:56, i * LANES : (i + 1) * LANES]
            num_box[0, slot, DIMS : DIMS + 1, :] = local[i][0:1, :]

            @pl.when(slot != 0)
            def _():
                remote(num_box.at[0, slot], num_box.at[1, slot], num_sems.at[0], num_sems.at[1], (dz, 0, 0, dc)).start()

        return 0

    lax.fori_loop(0, Z_CHIPS, ancestors_of, 0)

    g = col_end(last)
    g_box[x] = jnp.where(c == 0, g[0:Z_CHIPS], g[Z_CHIPS:])
    g_copies = [remote(g_box.at[x], g_box.at[x], g_sems.at[0], g_sems.at[1], d) for d in OVER_X]
    for copy in g_copies:
        copy.start()

    f_copy.wait_recv()
    f_here = f_box[jnp.where(half == c, 0, 1)]
    f_here = jnp.where(lax.rem(x, 2) == 0, f_here[0:4], f_here[4:8])
    block = src[...]
    norms = jnp.sum(block * block, axis=0, keepdims=True)
    count_here = count_src[at_src]
    lane = lax.broadcasted_iota(jnp.int32, (1, LANES), 1)
    for b in range(4):
        line = f_here[b : b + 1, :] * (1.0 / SCALE) + norms[:, b * LANES : (b + 1) * LANES]
        f_out[:, b * LANES : (b + 1) * LANES] = jnp.where(b * LANES + lane < count_here, line, 0.0)

    g_some = remote(g_box.at[pl.ds(0, 3)], g_box.at[pl.ds(0, 3)], g_sems.at[0], g_sems.at[1], OVER_X[0])
    g_some.wait_recv()
    g_some.wait_send()
    count_tile = count_tgt[at_tgt]
    for k in range(Z_CHIPS):
        for i in range(X_CHIPS):
            b = k * X_CHIPS + i
            block = tgt[:, b * LANES : (b + 1) * LANES]
            line = g_box[i, k : k + 1, :] * (1.0 / SCALE) + jnp.sum(block * block, axis=0, keepdims=True)
            g_out[:, b * LANES : (b + 1) * LANES] = jnp.where(b * LANES + lane < count_tile, line, 0.0)

    num_all = remote(
        num_box.at[1, pl.ds(1, 15)], num_box.at[1, pl.ds(1, 15)], num_sems.at[0], num_sems.at[1], OTHER_CORE
    )
    num_all.wait_recv()
    parts = [num_box.at[0, 0]] + [num_box.at[1, r] for r in range(1, 16)]
    weigh = [p[DIMS : DIMS + 1, :] for p in parts]
    total = log_sum(weigh)
    acc = jnp.zeros((DIMS, LANES), jnp.float32)
    for p, w in zip(parts, weigh):
        acc += p[0:DIMS, :] * jnp.exp2(w - total)
    anc_out[...] = jnp.where(at_src * LANES + lane < count_tile, acc, 0.0)

    num_all.wait_send()
    f_copy.wait_send()
    y_copy.wait_send()

    @pl.when(half == c)
    def _():
        for copy in x_copies:
            copy.wait_send()

    def sent(it, _):
        row_all(it).wait_send()
        col_all(it).wait_send()
        return 0

    lax.fori_loop(0, ITERS, sent, 0)


def shards(sources, targets, pair_active, count_src, count_tgt):
    f32, bf16 = jnp.float32, jnp.bfloat16
    vmem, sem = pltpu.VMEM, pltpu.SemaphoreType.DMA
    in_vmem = pl.BlockSpec(memory_space=pltpu.VMEM)
    in_smem = pl.BlockSpec(memory_space=pltpu.SMEM)
    f, g, anc = pl.pallas_call(
        kernel,
        out_shape=(
            jax.ShapeDtypeStruct((1, 512), f32),
            jax.ShapeDtypeStruct((1, 4096), f32),
            jax.ShapeDtypeStruct((DIMS, LANES), f32),
        ),
        in_specs=[in_smem, in_smem, in_smem, in_vmem, in_vmem],
        out_specs=(in_vmem, in_vmem, in_vmem),
        scratch_shapes=[
            vmem((X_CHIPS * CORES, 1, LANES), f32),
            vmem((2, DIMS, 512), f32),
            vmem((CORES, DIMS, COLS // 2), f32),
            vmem((PAD, ROWS), f32),
            vmem((PAD, COLS), f32),
            vmem((6 * PAD, ROWS), bf16),
            vmem((ROWS, 6 * PAD), bf16),
            vmem((6 * PAD, COLS), bf16),
            vmem((2 * PAD, ROWS), bf16),
            vmem((ROWS, COLS), f32),
            vmem((ROWS, LANES), f32),
            vmem((ROWS, LANES), f32),
            vmem((ROWS, LANES), f32),
            vmem((COL_BLOCKS, 8, LANES), f32),
            vmem((COL_BLOCKS, 8, LANES), f32),
            vmem((COL_BLOCKS, 8, LANES), f32),
            vmem((ITERS, 16, ROW_BLOCKS, LANES), f32),
            vmem((ITERS, 16, COL_BLOCKS, LANES), f32),
            vmem((2, ROW_BLOCKS, LANES), f32),
            vmem((X_CHIPS, Z_CHIPS, LANES), f32),
            vmem((2, 16, 56, LANES), f32),
            sem((2,)), sem(()), sem((2,)), sem((2,)), sem((ITERS,)), sem((ITERS,)), sem((ITERS,)), sem((ITERS,)),
            sem((2,)), sem((2,)), sem((2,)),
        ],
        compiler_params=pltpu.CompilerParams(
            collective_id=0, has_side_effects=True, vmem_limit_bytes=40 * 2**20
        ),
    )(count_src, count_tgt, pair_active, sources, targets)
    return f.reshape(512), g.reshape(4096), anc


def solution(mesh):
    return jax.shard_map(
        shards,
        mesh=mesh,
        in_specs=(P(None, "src"), P(None, "tgt"), P("src", "tgt"), P(), P()),
        out_specs=(P("src"), P("tgt"), P(None, ("tgt", "src"))),
        check_vma=False,
    )
```

time: 1480 us -> 99.8 us (0.07)
  blocking collectives: 1160 us -> 0 us
  waiting for transfers between devices: 192 us -> 0 us
  Pallas kernels: 0 us -> 94.4 us
  other arithmetic: 85.2 us -> 0 us
  matrix products: 23.9 us -> 0 us
  between operations: 16.2 us -> 1.35 us
    pmax x8 -> x0, blocking collectives: 665 us -> none  [the longest x4 447 us: shards(): best = lax.pmax(peak, 'src')]
    psum x8 -> x0, blocking collectives: 492 us -> none  [the longest x4 442 us: shards(): total = lax.psum(total * jnp.exp(peak - best), 'src')]
    psum x1 -> x0, waiting for transfers between devices: 192 us -> none  [shards(): summed = lax.psum(whole, 'src')]
    pallas_call x0 -> x1, Pallas kernels: none -> 94.4 us  [shards(): pl.pallas_call(kernel, out_shape=(jax.ShapeDtypeStruct((1, 512), f32), ja...]
    reduce_sum x12 -> x0, other arithmetic: 47.3 us -> none  [the longest x4 21.4 us: shards(): jnp.sum(jnp.where(allowed, jnp.exp(logits - peak[:, None]), 0.0), axis=1)]
    reduce_max x7 -> x0, other arithmetic: 31.3 us -> none  [the longest x4 17.8 us: shards(): peak = jnp.max(logits, axis=0)]
    dot_general x2 -> x0, matrix products: 23.9 us -> none  [the longest x1 12.3 us: shards(): lax.dot_general(sources, targets, (((0,), (0,)), ((), ())), precision=lax...]
  transfers between devices with their start and end apart: 1 -> 0, of which waited for: 1 -> 0; matrix products, arithmetic and copies ran while one was open for 0% -> 0% of each run, Pallas kernels for 0% -> 0%
where the time goes in v1:
time: 99.8 us; the launch traced here: 99.6 us
  Pallas kernels  94.4 us (95%)
  local copies, waits for them, and re-layouts  3.87 us (4%)
  between operations  1.35 us (1%)
    pallas_call x1, Pallas kernels, shards(): pl.pallas_call(kernel, out_shape=(jax.ShapeDtypeStruct((1, 512), f32), ja...  94.4 us
    unnamed x11, local copies, waits for them, and re-layouts  3.87 us

profile of v1, /device:TPU:1, one launch (start us, length us, event | category | flops | bytes accessed | tf_op | source)
XLA Modules:
  0.0 99.6 jit_solution(13775998148609482261)
XLA Ops:
  0.6 0.0 copy-start.3
  0.6 0.0 copy-start.2
  1.3 0.0 copy-done.3
  1.3 0.0 copy-done.2
  1.3 0.0 copy-start
  1.3 1.2 %copy-done = f32[50,4096]{1,0:T(8,128)S(1)} copy-done((f32[50,4096]{1,0:T(8,128)S(1)}, f32[50,4096]{1,0:T(8,128)}, u32[]{:S(2)}) %copy-start) | copy-done | bytes 819224
  2.5 0.0 copy-start.1
  2.5 0.9 copy-done.1
  3.4 94.4 %shard_map.76 = (f32[1,512]{1,0:T(1,128)S(1)}, f32[1,4096]{1,0:T(1,128)S(1)}, f32[50,128]{1,0:T(8,128)S(1)}) custom-call(s32[32]{0:T(128)S(1)} %copy-done.2, s32[8]{0:T(128)S(1)} %copy-done.3, s32[1,1]{1,0:T(1,128)S(6)} %copy.11.pair, f32[50,512]{1,0:T(8,128)S(1)} %copy-done.1, f32[50,4096]{1,0:T(8,128)S(1)} %copy-done), custom_call_target="tpu_custom_call" | custom-call | tf_op jit(solution)/shard_map/pallas_call | solution.py:387
  97.8 0.6 copy.12
  98.4 0.6 copy.13
  99.0 0.6 copy.14
Async XLA Ops:
  0.6 0.7 copy-start.3
  0.6 0.7 copy-start.2
  1.3 1.2 %copy-start = (f32[50,4096]{1,0:T(8,128)S(1)}, f32[50,4096]{1,0:T(8,128)}, u32[]{:S(2)}) copy-start(f32[50,4096]{1,0:T(8,128)} %tgt.1) | copy-start | bytes 2457604
  2.5 0.9 copy-start.1

commit v2 on v1

v2 whole, which is shorter than its diff:
```python
import math

import jax
import jax.numpy as jnp
from jax import lax
from jax.experimental import pallas as pl
from jax.experimental.pallas import tpu as pltpu
from jax.sharding import PartitionSpec as P

ITERS = 4
EPS = 0.02
SCALE = math.log2(math.e) / EPS
NEG = -(2.0**100)
LOW = -3.0e38
MESH = pl.DeviceIdType.MESH

DIMS = 50
PAD = 64
EXTRA = 16
ROWS = 1024
COLS = 2048
LANES = 128
COL_BLOCKS = COLS // LANES
X_CHIPS = 4
Y_CHIPS = 4
Z_CHIPS = 8
CORES = 2

OVER_XY = sorted(
    [(0, dx, dy, 0) for dx in range(X_CHIPS) for dy in range(Y_CHIPS) if dx or dy],
    key=lambda d: -(min(d[1], X_CHIPS - d[1]) + min(d[2], Y_CHIPS - d[2])),
)
OVER_Z_CORE = sorted(
    [(dz, 0, 0, dc) for dz in range(Z_CHIPS) for dc in range(CORES) if dz or dc],
    key=lambda d: -min(d[0], Z_CHIPS - d[0]),
)
OVER_X_CORE = [(0, dx, 0, dc) for dx in range(X_CHIPS) for dc in range(CORES) if dx or dc]
OVER_X = [(0, 2, 0, 0), (0, 1, 0, 0), (0, 3, 0, 0)]
OTHER_CORE = (0, 0, 0, 1)
PARTNERS = OVER_XY + OVER_Z_CORE + [d for d in OVER_X_CORE if d[1] and d[3]]


def tree(op, parts):
    while len(parts) > 1:
        parts = [op(*parts[i : i + 2]) if i + 1 < len(parts) else parts[i] for i in range(0, len(parts), 2)]
    return parts[0]


def log_sum(parts):
    peak = tree(jnp.maximum, parts)
    total = tree(jnp.add, [jnp.exp2(p - peak) for p in parts])
    return peak + jnp.log2(total)


def split(value, pieces):
    out = []
    for _ in range(pieces):
        piece = value.astype(jnp.bfloat16)
        out.append(piece)
        value = value - piece.astype(jnp.float32)
    return out


def kernel(
    count_src, count_tgt, pair, src, tgt,
    f_out, g_out, anc_out,
    x_own, flags, x_in, y_in, x_full, y_full, x_stack, x_lines, y_stack, x_pieces, y_norms,
    logits, row_peak, row_total, f_rep, g_rep, col_peak, col_total,
    row_box, col_box, f_box, g_box, num_own, num_give, num_got, num_send, num_in,
    own_sems, flag_sems, x_send, x_recv, y_sems, row_send, row_recv, col_send, col_recv, pair_sems, f_sems, g_sems,
    give_send, give_recv, num_sems,
):
    at_src = lax.axis_index("src")
    at_tgt = lax.axis_index("tgt")
    z, x = at_src // X_CHIPS, lax.rem(at_src, X_CHIPS)
    y, c = at_tgt // CORES, lax.rem(at_tgt, CORES)
    half = x // 2

    def device(d):
        dz, dx, dy, dc = d
        return (
            lax.rem(z + dz, Z_CHIPS) * X_CHIPS + lax.rem(x + dx, X_CHIPS),
            lax.rem(y + dy, Y_CHIPS) * CORES + lax.rem(c + dc, CORES),
        )

    def remote(a, b, send, recv, d):
        return pltpu.make_async_remote_copy(
            src_ref=a, dst_ref=b, send_sem=send, recv_sem=recv, device_id=device(d), device_id_type=MESH
        )

    def lanes(k, width=LANES):
        return pl.ds(pl.multiple_of(k * width, width), width)

    barrier = pltpu.get_barrier_semaphore()
    for d in PARTNERS:
        pl.semaphore_signal(barrier, inc=1, device_id=device(d), device_id_type=MESH)

    x_local = pltpu.make_async_copy(src, x_own, own_sems.at[0])
    x_local.start()
    y_local = [
        pltpu.make_async_copy(tgt.at[:, lanes(k * X_CHIPS + x)], y_in.at[c, :, lanes(k)], own_sems.at[1 + k])
        for k in range(Z_CHIPS)
    ]
    for copy in y_local:
        copy.start()
    mine = x * CORES + c
    listed = (pair[0, 0] > 0).astype(jnp.float32)
    flags[mine] = jnp.full((1, LANES), listed, jnp.float32)
    x_local.wait()
    for copy in y_local:
        copy.wait()
    pl.semaphore_wait(barrier, len(PARTNERS))

    x_copies = [remote(x_own, x_in.at[lax.rem(x, 2)], x_send, x_recv.at[lax.rem(x, 2)], d) for d in OVER_X]

    @pl.when(half == c)
    def _():
        for copy in x_copies:
            copy.start()

    y_copy = remote(y_in.at[c], y_in.at[c], y_sems.at[0], y_sems.at[1], OTHER_CORE)
    y_copy.start()
    for d in OVER_X_CORE:
        remote(flags.at[mine], flags.at[mine], flag_sems.at[0], flag_sems.at[1], d).start()

    def number_of(counts, length):
        total = counts[0]
        for i in range(1, length):
            total = total + counts[i]
        return total.astype(jnp.float32)

    log_a = -jnp.log2(jnp.full((4, LANES), number_of(count_src, Z_CHIPS * X_CHIPS), jnp.float32))
    log_b = -jnp.log2(jnp.full((COL_BLOCKS, LANES), number_of(count_tgt, Y_CHIPS * CORES), jnp.float32))
    col_counts = [count_tgt[y * CORES + i] for i in range(CORES)]

    def places(shape):
        return lax.broadcasted_iota(jnp.int32, shape, 0), lax.broadcasted_iota(jnp.int32, shape, 1)

    def row_live(h):
        block, lane = places((4, LANES))
        return block * LANES + lane < count_src[z * X_CHIPS + 2 * c + h]

    block, lane = places((COL_BLOCKS, LANES))
    within = (lax.rem(block, Z_CHIPS) * X_CHIPS + x) * LANES + lane
    col_live = within < jnp.where(block < Z_CHIPS, col_counts[0], col_counts[1])

    x_full[DIMS:PAD, :] = jnp.zeros((PAD - DIMS, ROWS), jnp.float32)
    y_full[DIMS:PAD, :] = jnp.zeros((PAD - DIMS, COLS), jnp.float32)

    def columns_of(tile):
        y_full[0:DIMS, lanes(tile, COLS // 2)] = y_in[tile]

        def body(k, _):
            b = tile * Z_CHIPS + k
            whole = y_full[:, lanes(b)]
            norm = jnp.sum(whole * whole, axis=0, keepdims=True)
            y_norms[b] = norm
            g_rep[b] = jnp.broadcast_to(-SCALE * norm, (8, LANES))
            p1, p2, p3 = split(whole, 3)
            for i, p in enumerate((p1, p2, p1, p3, p1, p2)):
                y_stack[i * PAD : (i + 1) * PAD, lanes(b)] = p
            return 0

        lax.fori_loop(0, Z_CHIPS, body, 0)

    columns_of(c)
    y_copy.wait_recv()
    columns_of(1 - c)
    flag_some = flags.at[pl.ds(0, len(OVER_X_CORE))]
    flag_all = remote(flag_some, flag_some, flag_sems.at[0], flag_sems.at[1], OTHER_CORE)
    flag_all.wait_recv()
    line, lane = places((EXTRA, LANES))
    for b in range(COL_BLOCKS):
        tile, k = b // Z_CHIPS, b % Z_CHIPS
        dead = jnp.where((k * X_CHIPS + x) * LANES + lane < col_counts[tile], 0.0, NEG)
        rows = [jnp.minimum(jnp.where(flags[(2 * c + i) * CORES + tile] > 0, 0.0, NEG), dead) for i in range(2)]
        extra = jnp.where(line == 0, rows[0], jnp.where(line == 1, rows[1], jnp.where(line == 2, 1.0, 0.0)))
        y_stack[6 * PAD :, b * LANES : (b + 1) * LANES] = extra.astype(jnp.bfloat16)

    def rows_of(h):
        live = count_src[z * X_CHIPS + 2 * c + h]
        x_full[0:DIMS, lanes(h, 512)] = x_in[h]
        for b in range(4):
            at = lanes(4 * h + b)
            whole = x_full[:, at]
            q1, q2 = split(whole, 2)
            x_pieces[0:PAD, at] = q1
            x_pieces[PAD:, at] = q2
            p1, p2, p3 = split(whole * (2.0 * SCALE), 3)
            for i, p in enumerate((p1, p1, p2, p1, p3, p2)):
                x_stack[i * PAD : (i + 1) * PAD, at] = p
            dead = jnp.where(b * LANES + lane < live, 0.0, NEG)
            extra = jnp.where(line == 2, dead, jnp.where(line == h, 1.0, 0.0))
            x_stack[6 * PAD :, at] = extra.astype(jnp.bfloat16)
            x_lines[at, :] = x_stack[:, at].T

        def logits_of(k, _):
            logits[lanes(h, 512), lanes(k, 256)] = jnp.dot(
                x_lines[lanes(h, 512), :], y_stack[:, lanes(k, 256)], preferred_element_type=jnp.float32
            )
            return 0

        lax.fori_loop(0, COLS // 256, logits_of, 0)

    def row_all(it, h):
        some = row_box.at[it, h, pl.ds(0, len(OVER_XY))]
        return remote(some, some, row_send.at[it, h], row_recv.at[it, h], OVER_XY[0])

    def row_start(it, h):
        def body(k, _):
            base = h * 512 + k * LANES
            for part in range(2):
                g = [g_rep[b] for b in range(part * 8, part * 8 + 8)]
                for q in range(16):
                    at = pl.ds(pl.multiple_of(base + 8 * q, 8), 8)
                    parts = [logits[at, (part * 8 + b) * LANES : (part * 8 + b + 1) * LANES] + g[b] for b in range(8)]
                    best = tree(jnp.maximum, parts)
                    if part:
                        peak = row_peak[at, :]
                        best = jnp.maximum(best, peak)
                    total = tree(jnp.add, [jnp.exp2(p - best) for p in parts])
                    if part:
                        total += row_total[at, :] * jnp.exp2(peak - best)
                    row_peak[at, :] = best
                    row_total[at, :] = total
            return 0

        lax.fori_loop(0, 4, body, 0)
        own = row_box.at[it, h, len(OVER_XY)]
        for b in range(4):
            peaks = row_peak[lanes(4 * h + b), :].T
            totals = row_total[lanes(4 * h + b), :].T
            peak = jnp.max(peaks, axis=0, keepdims=True)
            total = jnp.sum(totals * jnp.exp2(peaks - peak), axis=0, keepdims=True)
            own[b : b + 1, :] = peak + jnp.log2(total)
        for r, d in enumerate(OVER_XY):
            remote(own, row_box.at[it, h, r], row_send.at[it, h], row_recv.at[it, h], d).start()

    def row_end(it, h):
        row_all(it, h).wait_recv()
        total = log_sum([row_box[it, h, r] for r in range(len(OVER_XY) + 1)])
        f = jnp.where(row_live(h), log_a - total, 0.0)
        for b in range(4):
            f_rep[lanes(4 * h + b), :] = jnp.broadcast_to(f[b : b + 1, :], (LANES, LANES)).T
        return f

    def col_sums(h):
        def body(k, _):
            base = h * 512 + k * 64
            f = [f_rep[pl.ds(pl.multiple_of(base + 8 * j, 8), 8), :] for j in range(8)]
            for b in range(COL_BLOCKS):
                parts = [
                    logits[pl.ds(pl.multiple_of(base + 8 * j, 8), 8), b * LANES : (b + 1) * LANES] + f[j]
                    for j in range(8)
                ]
                peak = col_peak[b]
                best = jnp.maximum(peak, tree(jnp.maximum, parts))
                fresh = tree(jnp.add, [jnp.exp2(p - best) for p in parts])
                col_total[b] = col_total[b] * jnp.exp2(peak - best) + fresh
                col_peak[b] = best
            return 0

        lax.fori_loop(0, 8, body, 0, unroll=4)

    def col_reset():
        col_peak[...] = jnp.full((COL_BLOCKS, 8, LANES), LOW, jnp.float32)
        col_total[...] = jnp.zeros((COL_BLOCKS, 8, LANES), jnp.float32)

    def col_start(it):
        own = col_box.at[it, len(OVER_Z_CORE)]
        peaks = col_peak[...]
        peak = jnp.max(peaks, axis=1, keepdims=True)
        total = jnp.sum(col_total[...] * jnp.exp2(peaks - peak), axis=1)
        own[...] = peak[:, 0, :] + jnp.log2(total)
        return own

    def col_all(it, count):
        some = col_box.at[it, pl.ds(0, count)]
        return remote(some, some, col_send.at[it], col_recv.at[it], OVER_Z_CORE[0])

    def col_value(it):
        total = log_sum([col_box[it, r] for r in range(len(OVER_Z_CORE) + 1)])
        return jnp.where(col_live, log_b - total, 0.0)

    for k in range(2):
        h = lax.rem(k + x, 2)

        @pl.when(x == 2 * c + h)
        def _():
            x_in[h] = x_own[...]

        @pl.when(x != 2 * c + h)
        def _():
            remote(x_in.at[h], x_in.at[h], x_send, x_recv.at[h], OVER_X[0]).wait_recv()

        rows_of(h)
        row_start(0, h)

    def iteration(it, _):
        col_reset()
        for h in range(2):
            row_end(it, h)
            col_sums(h)
        own = col_start(it)
        for r, d in enumerate(OVER_Z_CORE):
            remote(own, col_box.at[it, r], col_send.at[it], col_recv.at[it], d).start()
        col_all(it, len(OVER_Z_CORE)).wait_recv()
        g = col_value(it)
        for b in range(COL_BLOCKS):
            g_rep[b] = jnp.broadcast_to(g[b : b + 1, :], (8, LANES))
        for h in range(2):
            row_start(it + 1, h)
        return 0

    last = ITERS - 1
    lax.fori_loop(0, last, iteration, 0)
    col_reset()
    for h in range(2):
        f_box[0, h] = row_end(last, h)
        col_sums(h)
    own = col_start(last)
    other = len(OVER_Z_CORE) - 1
    pair_copy = remote(own, col_box.at[last, other], pair_sems.at[0], pair_sems.at[1], OTHER_CORE)
    pair_copy.start()
    for r, d in enumerate(OVER_Z_CORE[:other]):
        remote(own, col_box.at[last, r], col_send.at[last], col_recv.at[last], d).start()
    f_copy = remote(f_box.at[0], f_box.at[1], f_sems.at[0], f_sems.at[1], OTHER_CORE)
    f_copy.start()
    pair_copy.wait_recv()
    both = log_sum([own[...], col_box[last, other]])
    for b in range(COL_BLOCKS):
        col_peak[b] = jnp.broadcast_to(both[b : b + 1, :], (8, LANES))

    def distance(k):
        step = (k + 1) // 2
        return jnp.where(lax.rem(k, 2) == 0, 4 + step, 4 - step)

    def give(k):
        return remote(num_give.at[k], num_got.at[k], give_send, give_recv.at[k], OTHER_CORE)

    def ancestors_of(k, _):
        @pl.when(k < Z_CHIPS)
        def _():
            to = lax.rem(z + distance(k), Z_CHIPS)
            cols = [lanes(i * Z_CHIPS + to) for i in range(CORES)]
            local = [col_peak[i * Z_CHIPS + to] for i in range(CORES)]
            acc = jnp.zeros((PAD, CORES * LANES), jnp.float32)
            for r in range(ROWS // 256):
                at = slice(r * 256, (r + 1) * 256)
                f = f_rep[at, :]
                weight = jnp.concatenate(
                    [jnp.exp2(logits[at, cols[i]] + (f - local[i][0:1, :])) for i in range(CORES)], axis=1
                )
                w1, w2 = split(weight, 2)
                two = jnp.dot(x_pieces[:, at], w1, preferred_element_type=jnp.float32)
                acc += two[0:PAD] + two[PAD:] + jnp.dot(x_pieces[0:PAD, at], w2, preferred_element_type=jnp.float32)
            tiles = [acc[0:56, i * LANES : (i + 1) * LANES] for i in range(CORES)]
            num_own[k] = jnp.where(c == 0, tiles[0], tiles[1])
            num_give[k] = jnp.where(c == 0, tiles[1], tiles[0])
            give(k).start()

        @pl.when(k >= 2)
        def _():
            j = k - 2
            dz = distance(j)
            give(j).wait_recv()
            num_send[j] = num_own[j] + num_got[j]
            num_send[j, DIMS : DIMS + 1, :] = col_peak[c * Z_CHIPS + lax.rem(z + dz, Z_CHIPS)][0:1, :]

            @pl.when(j < Z_CHIPS - 1)
            def _():
                remote(num_send.at[j], num_in.at[j], num_sems.at[0], num_sems.at[1], (dz, 0, 0, 0)).start()

        return 0

    lax.fori_loop(0, Z_CHIPS + 2, ancestors_of, 0)

    col_all(last, other).wait_recv()
    g = col_value(last)
    g_here = jnp.where(c == 0, g[0:Z_CHIPS], g[Z_CHIPS:]) * (1.0 / SCALE)
    for k in range(Z_CHIPS):
        norm = y_norms[c * Z_CHIPS + k]
        within = (k * X_CHIPS + x) * LANES + lax.broadcasted_iota(jnp.int32, (1, LANES), 1)
        g_box[x, k : k + 1, :] = jnp.where(within < count_tgt[at_tgt], g_here[k : k + 1, :] + norm, 0.0)
    for d in OVER_X:
        remote(g_box.at[x], g_box.at[x], g_sems.at[0], g_sems.at[1], d).start()

    f_copy.wait_recv()
    f_here = f_box[jnp.where(half == c, 0, 1), lax.rem(x, 2)]
    block = x_own[...]
    norms = jnp.sum(block * block, axis=0, keepdims=True)
    count_here = count_src[at_src]
    lane = lax.broadcasted_iota(jnp.int32, (1, LANES), 1)
    for b in range(4):
        value = f_here[b : b + 1, :] * (1.0 / SCALE) + norms[:, b * LANES : (b + 1) * LANES]
        f_out[:, b * LANES : (b + 1) * LANES] = jnp.where(b * LANES + lane < count_here, value, 0.0)

    some = num_in.at[pl.ds(0, Z_CHIPS - 1)]
    num_all = remote(some, some, num_sems.at[0], num_sems.at[1], OVER_Z_CORE[0])
    num_all.wait_recv()
    parts = [num_in.at[r] for r in range(Z_CHIPS - 1)] + [num_send.at[Z_CHIPS - 1]]
    weigh = [p[DIMS : DIMS + 1, :] for p in parts]
    total = log_sum(weigh)
    acc = jnp.zeros((DIMS, LANES), jnp.float32)
    for p, w in zip(parts, weigh):
        acc += p[0:DIMS, :] * jnp.exp2(w - total)
    anc_out[...] = jnp.where(at_src * LANES + lane < count_tgt[at_tgt], acc, 0.0)

    g_some = remote(g_box.at[pl.ds(0, 3)], g_box.at[pl.ds(0, 3)], g_sems.at[0], g_sems.at[1], OVER_X[0])
    g_some.wait_recv()
    for k in range(Z_CHIPS):
        for i in range(X_CHIPS):
            b = k * X_CHIPS + i
            g_out[:, b * LANES : (b + 1) * LANES] = g_box[i, k : k + 1, :]

    num_all.wait_send()
    g_some.wait_send()
    f_copy.wait_send()
    y_copy.wait_send()
    flag_all.wait_send()
    pair_copy.wait_send()
    remote(num_give, num_got, give_send, give_recv.at[0], OTHER_CORE).wait_send()

    @pl.when(half == c)
    def _():
        for copy in x_copies:
            copy.wait_send()

    def sent(it, _):
        row_all(it, 0).wait_send()
        row_all(it, 1).wait_send()
        return 0

    lax.fori_loop(0, ITERS, sent, 0)
    for it in range(ITERS):
        col_all(it, len(OVER_Z_CORE) if it < last else other).wait_send()


def shards(sources, targets, pair_active, count_src, count_tgt):
    f32, bf16 = jnp.float32, jnp.bfloat16
    vmem, sem = pltpu.VMEM, pltpu.SemaphoreType.DMA
    in_vmem = pl.BlockSpec(memory_space=pltpu.VMEM)
    in_smem = pl.BlockSpec(memory_space=pltpu.SMEM)
    in_place = pl.BlockSpec(memory_space=pl.ANY)
    f, g, anc = pl.pallas_call(
        kernel,
        out_shape=(
            jax.ShapeDtypeStruct((1, 512), f32),
            jax.ShapeDtypeStruct((1, 4096), f32),
            jax.ShapeDtypeStruct((DIMS, LANES), f32),
        ),
        in_specs=[in_smem, in_smem, in_smem, in_place, in_place],
        out_specs=(in_vmem, in_vmem, in_vmem),
        scratch_shapes=[
            vmem((DIMS, 512), f32),
            vmem((X_CHIPS * CORES, 1, LANES), f32),
            vmem((2, DIMS, 512), f32),
            vmem((CORES, DIMS, COLS // 2), f32),
            vmem((PAD, ROWS), f32),
            vmem((PAD, COLS), f32),
            vmem((6 * PAD + EXTRA, ROWS), bf16),
            vmem((ROWS, 6 * PAD + EXTRA), bf16),
            vmem((6 * PAD + EXTRA, COLS), bf16),
            vmem((2 * PAD, ROWS), bf16),
            vmem((COL_BLOCKS, 1, LANES), f32),
            vmem((ROWS, COLS), f32),
            vmem((ROWS, LANES), f32),
            vmem((ROWS, LANES), f32),
            vmem((ROWS, LANES), f32),
            vmem((COL_BLOCKS, 8, LANES), f32),
            vmem((COL_BLOCKS, 8, LANES), f32),
            vmem((COL_BLOCKS, 8, LANES), f32),
            vmem((ITERS, 2, 16, 4, LANES), f32),
            vmem((ITERS, 16, COL_BLOCKS, LANES), f32),
            vmem((2, 2, 4, LANES), f32),
            vmem((X_CHIPS, Z_CHIPS, LANES), f32),
            vmem((Z_CHIPS, 56, LANES), f32),
            vmem((Z_CHIPS, 56, LANES), f32),
            vmem((Z_CHIPS, 56, LANES), f32),
            vmem((Z_CHIPS, 56, LANES), f32),
            vmem((Z_CHIPS, 56, LANES), f32),
            sem((1 + Z_CHIPS,)), sem((2,)), sem(()), sem((2,)), sem((2,)), sem((ITERS, 2)), sem((ITERS, 2)),
            sem((ITERS,)), sem((ITERS,)), sem((2,)), sem((2,)), sem((2,)), sem(()), sem((Z_CHIPS,)), sem((2,)),
        ],
        compiler_params=pltpu.CompilerParams(
            collective_id=0, has_side_effects=True, vmem_limit_bytes=40 * 2**20
        ),
    )(count_src, count_tgt, pair_active, sources, targets)
    return f.reshape(512), g.reshape(4096), anc


def solution(mesh):
    return jax.shard_map(
        shards,
        mesh=mesh,
        in_specs=(P(None, "src"), P(None, "tgt"), P("src", "tgt"), P(), P()),
        out_specs=(P("src"), P("tgt"), P(None, ("tgt", "src"))),
        check_vma=False,
    )
```

time: 99.8 us -> 83.6 us (0.84)
  Pallas kernels: 94.4 us -> 78.2 us
    pallas_call x1, Pallas kernels: 94.4 us -> 78.2 us  [shards(): pl.pallas_call(kernel, out_shape=(jax.ShapeDtypeStruct((1, 512), f32), ja...]
where the time goes in v2:
time: 83.6 us; the launch traced here: 83.5 us
  Pallas kernels  78.2 us (94%)
  local copies, waits for them, and re-layouts  3.87 us (5%)
  between operations  1.35 us (2%)
    pallas_call x1, Pallas kernels, shards(): pl.pallas_call(kernel, out_shape=(jax.ShapeDtypeStruct((1, 512), f32), ja...  78.2 us
    unnamed x11, local copies, waits for them, and re-layouts  3.87 us

profile of v2, /device:TPU:1, one launch (start us, length us, event | category | flops | bytes accessed | tf_op | source)
XLA Modules:
  0.0 83.5 jit_solution(17385248885725486207)
XLA Ops:
  0.6 0.0 copy-start.3
  0.6 0.0 copy-start.2
  1.3 0.0 copy-done.3
  1.3 0.0 copy-done.2
  1.3 0.0 copy-start
  1.3 1.2 %copy-done = f32[50,4096]{1,0:T(8,128)S(1)} copy-done((f32[50,4096]{1,0:T(8,128)S(1)}, f32[50,4096]{1,0:T(8,128)}, u32[]{:S(2)}) %copy-start) | copy-done | bytes 819224
  2.5 0.0 copy-start.1
  2.5 0.9 %copy-done.1 = f32[50,512]{1,0:T(8,128)S(1)} copy-done((f32[50,512]{1,0:T(8,128)S(1)}, f32[50,512]{1,0:T(8,128)}, u32[]{:S(2)}) %copy-start.1) | copy-done | bytes 102424
  3.4 78.2 %shard_map.76 = (f32[1,512]{1,0:T(1,128)S(1)}, f32[1,4096]{1,0:T(1,128)S(1)}, f32[50,128]{1,0:T(8,128)S(1)}) custom-call(s32[32]{0:T(128)S(1)} %copy-done.2, s32[8]{0:T(128)S(1)} %copy-done.3, s32[1,1]{1,0:T(1,128)S(6)} %copy.11.pair, f32[50,512]{1,0:T(8,128)S(1)} %copy-done.1, f32[50,4096]{1,0:T(8,128)S(1)} %copy-done), custom_call_target="tpu_custom_call" | custom-call | tf_op jit(solution)/shard_map/pallas_call | solution.py:445
  81.7 0.6 copy.12
  82.2 0.6 copy.13
  82.8 0.6 copy.14
Async XLA Ops:
  0.6 0.7 copy-start.3
  0.6 0.7 copy-start.2
  1.3 1.2 %copy-start = (f32[50,4096]{1,0:T(8,128)S(1)}, f32[50,4096]{1,0:T(8,128)}, u32[]{:S(2)}) copy-start(f32[50,4096]{1,0:T(8,128)} %tgt.1) | copy-start | bytes 2457604
  2.5 0.9 %copy-start.1 = (f32[50,512]{1,0:T(8,128)S(1)}, f32[50,512]{1,0:T(8,128)}, u32[]{:S(2)}) copy-start(f32[50,512]{1,0:T(8,128)} %src.1) | copy-start | bytes 307204

commit v3 on v2

v3 whole, which is shorter than its diff:
```python
import math

import jax
import jax.numpy as jnp
from jax import lax
from jax.experimental import pallas as pl
from jax.experimental.pallas import tpu as pltpu
from jax.sharding import PartitionSpec as P

ITERS = 4
EPS = 0.02
SCALE = math.log2(math.e) / EPS
NEG = -(2.0**100)
LOW = -3.0e38
LOGICAL = pl.DeviceIdType.LOGICAL

DIMS = 50
PAD = 64
EXTRA = 16
ROWS = 1024
COLS = 2048
LANES = 128
COL_BLOCKS = COLS // LANES
PARTS = 2
PART_BLOCKS = ROWS // LANES // PARTS
PART_ROWS = ROWS // PARTS
X_CHIPS = 4
Y_CHIPS = 4
Z_CHIPS = 8
CORES = 2

OVER_XY = sorted(
    [(0, dx, dy, 0) for dx in range(X_CHIPS) for dy in range(Y_CHIPS) if dx or dy],
    key=lambda d: -(min(d[1], X_CHIPS - d[1]) + min(d[2], Y_CHIPS - d[2])),
)
OVER_Z = sorted([(dz, 0, 0, 0) for dz in range(1, Z_CHIPS)], key=lambda d: -min(d[0], Z_CHIPS - d[0]))
OVER_X_CORE = [(0, dx, 0, dc) for dx in range(X_CHIPS) for dc in range(CORES) if dx or dc]
OVER_X = [(0, 2, 0, 0), (0, 1, 0, 0), (0, 3, 0, 0)]
OTHER_CORE = (0, 0, 0, 1)
PARTNERS = OVER_XY + OVER_Z + [OTHER_CORE] + [d for d in OVER_X_CORE if d[1] and d[3]]


def tree(op, parts):
    while len(parts) > 1:
        parts = [op(*parts[i : i + 2]) if i + 1 < len(parts) else parts[i] for i in range(0, len(parts), 2)]
    return parts[0]


def log_sum(parts):
    peak = tree(jnp.maximum, parts)
    total = tree(jnp.add, [jnp.exp2(p - peak) for p in parts])
    return peak + jnp.log2(total)


def split(value, pieces):
    out = []
    for _ in range(pieces):
        piece = value.astype(jnp.bfloat16)
        out.append(piece)
        value = value - piece.astype(jnp.float32)
    return out


def kernel(
    counts_src, counts_tgt, pairs, src, tgt,
    f_out, g_out, anc_out,
    count_src, count_tgt, pair, x_own, flags, x_in, y_in, x_full, y_full, y_stack, x_pieces, y_norms,
    logits, row_peak, row_total, f_rep, g_rep, col_peak, col_total,
    row_box, col_box, core_box, f_box, g_box, num_own, num_give, num_got, num_send, num_in,
    own_sems, flag_sems, x_send, x_recv, y_sems, row_send, row_recv, col_send, col_recv, core_send, core_recv, f_sems, g_sems,
    give_send, give_recv, num_sems,
):
    at_src = lax.axis_index("src")
    at_tgt = lax.axis_index("tgt")
    z, x = at_src // X_CHIPS, at_src & (X_CHIPS - 1)
    y, c = at_tgt // CORES, at_tgt & (CORES - 1)
    half = x // 2

    def device(d):
        dz, dx, dy, dc = d
        at_z = (z + dz) & (Z_CHIPS - 1) if not isinstance(dz, int) or dz else z
        at_x = (x + dx) & (X_CHIPS - 1) if dx else x
        at_y = (y + dy) & (Y_CHIPS - 1) if dy else y
        at_c = c ^ dc
        return ((at_z * X_CHIPS + at_x) * Y_CHIPS + at_y) * CORES + at_c

    ids = {d: device(d) for d in PARTNERS}

    def remote(a, b, send, recv, d):
        return pltpu.make_async_remote_copy(
            src_ref=a, dst_ref=b, send_sem=send, recv_sem=recv, device_id=ids[d] if isinstance(d[0], int) else device(d), device_id_type=LOGICAL
        )

    def lanes(k, width=LANES):
        return pl.ds(pl.multiple_of(k * width, width), width)

    barrier = pltpu.get_barrier_semaphore()
    for d in PARTNERS:
        pl.semaphore_signal(barrier, inc=1, device_id=ids[d], device_id_type=LOGICAL)

    x_local = [pltpu.make_async_copy(src.at[:, lanes(k)], x_own.at[k], own_sems.at[k]) for k in range(4)]
    for copy in x_local:
        copy.start()
    y_local = [
        pltpu.make_async_copy(tgt.at[:, lanes(k * X_CHIPS + x)], y_in.at[c, :, lanes(k)], own_sems.at[4 + k])
        for k in range(Z_CHIPS)
    ]
    for copy in y_local:
        copy.start()
    scalars = [
        pltpu.make_async_copy(a, b, own_sems.at[4 + Z_CHIPS + i])
        for i, (a, b) in enumerate(((counts_src, count_src), (counts_tgt, count_tgt), (pairs, pair)))
    ]
    for copy in scalars:
        copy.start()
    for copy in scalars:
        copy.wait()
    mine = x * CORES + c
    listed = (pair[0, 0] > 0).astype(jnp.float32)
    flags[mine] = jnp.full((1, LANES), listed, jnp.float32)
    for copy in x_local + y_local:
        copy.wait()
    pl.semaphore_wait(barrier, len(PARTNERS))

    x_copies = [
        remote(x_own.at[k], x_in.at[x & 1, k], x_send, x_recv.at[x & 1, k], d) for k in range(4) for d in OVER_X
    ]

    @pl.when(half == c)
    def _():
        for copy in x_copies:
            copy.start()

    y_copy = remote(y_in.at[c], y_in.at[c], y_sems.at[0], y_sems.at[1], OTHER_CORE)
    y_copy.start()
    for d in OVER_X_CORE:
        remote(flags.at[mine], flags.at[mine], flag_sems.at[0], flag_sems.at[1], d).start()

    def number_of(counts, length):
        total = counts[0]
        for i in range(1, length):
            total = total + counts[i]
        return total.astype(jnp.float32)

    log_a = -jnp.log2(jnp.full((PART_BLOCKS, LANES), number_of(count_src, Z_CHIPS * X_CHIPS), jnp.float32))
    log_b = -jnp.log2(jnp.full((Z_CHIPS, LANES), number_of(count_tgt, Y_CHIPS * CORES), jnp.float32))
    col_counts = [count_tgt[y * CORES + i] for i in range(CORES)]

    def places(shape):
        return lax.broadcasted_iota(jnp.int32, shape, 0), lax.broadcasted_iota(jnp.int32, shape, 1)

    def row_live(q):
        block, lane = places((PART_BLOCKS, LANES))
        within = (lax.rem(q * PART_BLOCKS, 4) + block) * LANES + lane
        return within < count_src[z * X_CHIPS + 2 * c + q * PART_BLOCKS // 4]

    block, lane = places((Z_CHIPS, LANES))
    col_within = (block * X_CHIPS + x) * LANES + lane
    col_live = [col_within < count for count in col_counts]

    x_full[DIMS:PAD, :] = jnp.zeros((PAD - DIMS, ROWS), jnp.float32)
    y_full[DIMS:PAD, :] = jnp.zeros((PAD - DIMS, COLS), jnp.float32)

    def columns_of(tile):
        y_full[0:DIMS, lanes(tile, COLS // 2)] = y_in[tile]

        def body(k, _):
            b = tile * Z_CHIPS + k
            whole = y_full[:, lanes(b)]
            norm = jnp.sum(whole * whole, axis=0, keepdims=True)
            y_norms[b] = norm
            g_rep[b] = jnp.broadcast_to(-SCALE * norm, (8, LANES))
            p1, p2, p3 = split(whole, 3)
            for i, p in enumerate((p1, p2, p1, p3, p1, p2)):
                y_stack[i * PAD : (i + 1) * PAD, lanes(b)] = p
            return 0

        lax.fori_loop(0, Z_CHIPS, body, 0)

    columns_of(c)
    y_copy.wait_recv()
    columns_of(1 - c)
    flag_some = flags.at[pl.ds(0, len(OVER_X_CORE))]
    flag_all = remote(flag_some, flag_some, flag_sems.at[0], flag_sems.at[1], OTHER_CORE)
    flag_all.wait_recv()
    line, lane = places((EXTRA, LANES))
    for b in range(COL_BLOCKS):
        tile, k = b // Z_CHIPS, b % Z_CHIPS
        dead = jnp.where((k * X_CHIPS + x) * LANES + lane < col_counts[tile], 0.0, NEG)
        rows = [jnp.minimum(jnp.where(flags[(2 * c + i) * CORES + tile] > 0, 0.0, NEG), dead) for i in range(2)]
        extra = jnp.where(line == 0, rows[0], jnp.where(line == 1, rows[1], jnp.where(line == 2, 1.0, 0.0)))
        y_stack[6 * PAD :, b * LANES : (b + 1) * LANES] = extra.astype(jnp.bfloat16)

    def rows_of(h, k):
        live = count_src[z * X_CHIPS + 2 * c + h]
        at = lanes(4 * h + k)
        x_full[0:DIMS, at] = x_in[h, k]
        whole = x_full[:, at]
        q1, q2 = split(whole, 2)
        x_pieces[0:PAD, at] = q1
        x_pieces[PAD:, at] = q2
        p1, p2, p3 = split(whole * (2.0 * SCALE), 3)
        dead = jnp.where(k * LANES + lane < live, 0.0, NEG)
        extra = jnp.where(line == 2, dead, jnp.where(line == h, 1.0, 0.0))
        stack = jnp.concatenate([p1, p1, p2, p1, p3, p2, extra.astype(jnp.bfloat16)], axis=0)
        rows = stack.T
        for i in range(COLS // 256):
            cols = slice(i * 256, (i + 1) * 256)
            logits[at, cols] = jnp.dot(rows, y_stack[:, cols], preferred_element_type=jnp.float32)

    def row_all(it, q):
        some = row_box.at[it, q, pl.ds(0, len(OVER_XY))]
        return remote(some, some, row_send.at[it, q], row_recv.at[it, q], OVER_XY[0])

    def row_sums_at(base, tile):
        g = [g_rep[tile * 8 + b] for b in range(8)]
        for i in range(16):
            at = pl.ds(pl.multiple_of(base + 8 * i, 8), 8)
            parts = [logits[at, (tile * 8 + b) * LANES : (tile * 8 + b + 1) * LANES] + g[b] for b in range(8)]
            best = tree(jnp.maximum, parts)
            if tile:
                peak = row_peak[at, :]
                best = jnp.maximum(best, peak)
            total = tree(jnp.add, [jnp.exp2(p - best) for p in parts])
            if tile:
                total += row_total[at, :] * jnp.exp2(peak - best)
            row_peak[at, :] = best
            row_total[at, :] = total

    def row_sums(q, tile):
        def body(k, _):
            row_sums_at(q * PART_ROWS + k * LANES, tile)
            return 0

        lax.fori_loop(0, PART_BLOCKS, body, 0)

    def row_start(it, q):
        own = row_box.at[it, q, len(OVER_XY)]
        for b in range(PART_BLOCKS):
            peaks = row_peak[lanes(PART_BLOCKS * q + b), :].T
            totals = row_total[lanes(PART_BLOCKS * q + b), :].T
            peak = jnp.max(peaks, axis=0, keepdims=True)
            total = jnp.sum(totals * jnp.exp2(peaks - peak), axis=0, keepdims=True)
            own[b : b + 1, :] = peak + jnp.log2(total)
        for r, d in enumerate(OVER_XY):
            remote(own, row_box.at[it, q, r], row_send.at[it, q], row_recv.at[it, q], d).start()

    def row_end(it, q):
        row_all(it, q).wait_recv()
        total = log_sum([row_box[it, q, r] for r in range(len(OVER_XY) + 1)])
        f = jnp.where(row_live(q), log_a - total, 0.0)
        for b in range(PART_BLOCKS):
            f_rep[lanes(PART_BLOCKS * q + b), :] = jnp.broadcast_to(f[b : b + 1, :], (LANES, LANES)).T
        return f

    def col_sums(q, tiles):
        def body(k, _):
            base = q * PART_ROWS + k * 64
            f = [f_rep[pl.ds(pl.multiple_of(base + 8 * j, 8), 8), :] for j in range(8)]
            for tile in tiles:
                for b in range(tile * 8, tile * 8 + 8):
                    parts = [
                        logits[pl.ds(pl.multiple_of(base + 8 * j, 8), 8), b * LANES : (b + 1) * LANES] + f[j]
                        for j in range(8)
                    ]
                    peak = col_peak[b]
                    best = jnp.maximum(peak, tree(jnp.maximum, parts))
                    fresh = tree(jnp.add, [jnp.exp2(p - best) for p in parts])
                    col_total[b] = col_total[b] * jnp.exp2(peak - best) + fresh
                    col_peak[b] = best
            return 0

        lax.fori_loop(0, PART_ROWS // 64, body, 0, unroll=4)

    def col_reset():
        col_peak[...] = jnp.full((COL_BLOCKS, 8, LANES), LOW, jnp.float32)
        col_total[...] = jnp.zeros((COL_BLOCKS, 8, LANES), jnp.float32)

    def col_sum(tile):
        peaks = col_peak[tile * 8 : tile * 8 + 8]
        peak = jnp.max(peaks, axis=1, keepdims=True)
        total = jnp.sum(col_total[tile * 8 : tile * 8 + 8] * jnp.exp2(peaks - peak), axis=1)
        return peak[:, 0, :] + jnp.log2(total)

    def col_give(it, tile, value):
        own = col_box.at[it, tile, len(OVER_Z)]
        own[...] = value
        for r, d in enumerate(OVER_Z):
            remote(own, col_box.at[it, tile, r], col_send.at[it, tile], col_recv.at[it, tile], d).start()

    def col_all(it, tile):
        some = col_box.at[it, tile, pl.ds(0, len(OVER_Z))]
        return remote(some, some, col_send.at[it, tile], col_recv.at[it, tile], OVER_Z[0])

    def over_z(it, tile):
        col_all(it, tile).wait_recv()
        return log_sum([col_box[it, tile, r] for r in range(len(OVER_Z) + 1)])

    def core_copy(it, tile):
        return remote(
            core_box.at[it, tile, 1], core_box.at[it, tile, 0], core_send.at[it, tile], core_recv.at[it, tile], OTHER_CORE
        )

    def core_give(it, tile, value):
        core_box[it, tile, 1] = value
        core_copy(it, tile).start()

    def over_cores(it, tile):
        core_copy(it, tile).wait_recv()
        return log_sum([core_box[it, tile, r] for r in range(2)])

    for i in range(2):
        h = (x & 1) ^ jnp.where(half == c, i, 1 - i)
        here = x == 2 * c + h

        @pl.when(here)
        def _():
            x_in[h] = x_own[...]

        def rows_and_sums(k, _):
            @pl.when(jnp.logical_not(here))
            def _():
                remote(x_in.at[h, k], x_in.at[h, k], x_send, x_recv.at[h, k], OVER_X[0]).wait_recv()

            rows_of(h, k)
            for tile in range(CORES):
                row_sums_at((4 * h + k) * LANES, tile)
            return 0

        lax.fori_loop(0, 4, rows_and_sums, 0)
        row_start(0, h)

    def columns_from_rows(it, give):
        col_reset()
        for q in range(PARTS):
            f_box[0, q] = row_end(it, q)
            if q < PARTS - 1:
                col_sums(q, (0, 1))
        for tile in range(CORES):
            col_sums(PARTS - 1, (tile,))
            give(it, tile, col_sum(tile))

    def iteration(it, _):
        columns_from_rows(it, col_give)
        for tile in range(CORES):
            core_give(it, tile, over_z(it, tile))
        for tile in range(CORES):
            g = jnp.where(col_live[tile], log_b - over_cores(it, tile), 0.0)
            for b in range(Z_CHIPS):
                g_rep[tile * Z_CHIPS + b] = jnp.broadcast_to(g[b : b + 1, :], (8, LANES))
            for q in range(PARTS):
                row_sums(q, tile)
                if tile == CORES - 1:
                    row_start(it + 1, q)
        return 0

    last = ITERS - 1
    lax.fori_loop(0, last, iteration, 0)
    columns_from_rows(last, core_give)
    f_copy = remote(f_box.at[0], f_box.at[1], f_sems.at[0], f_sems.at[1], OTHER_CORE)
    f_copy.start()
    both = [over_cores(last, tile) for tile in range(CORES)]
    col_give(last, 0, jnp.where(c == 0, both[0], both[1]))
    for tile in range(CORES):
        for b in range(Z_CHIPS):
            col_peak[tile * Z_CHIPS + b] = jnp.broadcast_to(both[tile][b : b + 1, :], (8, LANES))

    def distance(k):
        step = (k + 1) // 2
        return jnp.where(lax.rem(k, 2) == 0, 4 + step, 4 - step)

    def give(k):
        return remote(num_give.at[k], num_got.at[k], give_send, give_recv.at[k], OTHER_CORE)

    def ancestors_of(k, _):
        @pl.when(k < Z_CHIPS)
        def _():
            to = lax.rem(z + distance(k), Z_CHIPS)
            cols = [lanes(i * Z_CHIPS + to) for i in range(CORES)]
            local = [col_peak[i * Z_CHIPS + to] for i in range(CORES)]
            acc = jnp.zeros((PAD, CORES * LANES), jnp.float32)
            for r in range(ROWS // 256):
                at = slice(r * 256, (r + 1) * 256)
                f = f_rep[at, :]
                weight = jnp.concatenate(
                    [jnp.exp2(logits[at, cols[i]] + (f - local[i][0:1, :])) for i in range(CORES)], axis=1
                )
                w1, w2 = split(weight, 2)
                two = jnp.dot(x_pieces[:, at], w1, preferred_element_type=jnp.float32)
                acc += two[0:PAD] + two[PAD:] + jnp.dot(x_pieces[0:PAD, at], w2, preferred_element_type=jnp.float32)
            tiles = [acc[0:56, i * LANES : (i + 1) * LANES] for i in range(CORES)]
            num_own[k] = jnp.where(c == 0, tiles[0], tiles[1])
            num_give[k] = jnp.where(c == 0, tiles[1], tiles[0])
            give(k).start()

        @pl.when(k >= 2)
        def _():
            j = k - 2
            dz = distance(j)
            give(j).wait_recv()
            num_send[j] = num_own[j] + num_got[j]
            num_send[j, DIMS : DIMS + 1, :] = col_peak[c * Z_CHIPS + lax.rem(z + dz, Z_CHIPS)][0:1, :]

            @pl.when(j < Z_CHIPS - 1)
            def _():
                remote(num_send.at[j], num_in.at[j], num_sems.at[0], num_sems.at[1], (dz, 0, 0, 0)).start()

        return 0

    lax.fori_loop(0, Z_CHIPS + 2, ancestors_of, 0)

    live_here = col_within < count_tgt[at_tgt]
    g_here = jnp.where(live_here, (log_b - over_z(last, 0)) * (1.0 / SCALE), 0.0)
    for k in range(Z_CHIPS):
        norm = y_norms[c * Z_CHIPS + k]
        within = (k * X_CHIPS + x) * LANES + lax.broadcasted_iota(jnp.int32, (1, LANES), 1)
        g_box[x, k : k + 1, :] = jnp.where(within < count_tgt[at_tgt], g_here[k : k + 1, :] + norm, 0.0)
    for d in OVER_X:
        remote(g_box.at[x], g_box.at[x], g_sems.at[0], g_sems.at[1], d).start()

    f_copy.wait_recv()
    count_here = count_src[at_src]
    lane = lax.broadcasted_iota(jnp.int32, (1, LANES), 1)
    from_core = jnp.where(half == c, 0, 1)
    for b in range(4):
        at = lax.rem(x, 2) * 4 + b
        f_here = f_box[from_core, at // PART_BLOCKS, lax.rem(at, PART_BLOCKS)]
        value = f_here[None, :] * (1.0 / SCALE) + jnp.sum(x_own[b] * x_own[b], axis=0, keepdims=True)
        f_out[:, b * LANES : (b + 1) * LANES] = jnp.where(b * LANES + lane < count_here, value, 0.0)

    some = num_in.at[pl.ds(0, Z_CHIPS - 1)]
    num_all = remote(some, some, num_sems.at[0], num_sems.at[1], OVER_Z[0])
    num_all.wait_recv()
    parts = [num_in.at[r] for r in range(Z_CHIPS - 1)] + [num_send.at[Z_CHIPS - 1]]
    weigh = [p[DIMS : DIMS + 1, :] for p in parts]
    total = log_sum(weigh)
    acc = jnp.zeros((DIMS, LANES), jnp.float32)
    for p, w in zip(parts, weigh):
        acc += p[0:DIMS, :] * jnp.exp2(w - total)
    anc_out[...] = jnp.where(at_src * LANES + lane < count_tgt[at_tgt], acc, 0.0)

    g_some = remote(g_box.at[pl.ds(0, 3)], g_box.at[pl.ds(0, 3)], g_sems.at[0], g_sems.at[1], OVER_X[0])
    g_some.wait_recv()
    for k in range(Z_CHIPS):
        for i in range(X_CHIPS):
            b = k * X_CHIPS + i
            g_out[:, b * LANES : (b + 1) * LANES] = g_box[i, k : k + 1, :]

    num_all.wait_send()
    g_some.wait_send()
    f_copy.wait_send()
    y_copy.wait_send()
    flag_all.wait_send()
    remote(num_give, num_got, give_send, give_recv.at[0], OTHER_CORE).wait_send()

    @pl.when(half == c)
    def _():
        for copy in x_copies:
            copy.wait_send()

    def sent(it, _):
        for q in range(PARTS):
            row_all(it, q).wait_send()
        return 0

    lax.fori_loop(0, ITERS, sent, 0)
    for it in range(ITERS):
        for tile in range(CORES):
            core_copy(it, tile).wait_send()
            if it < last or tile == 0:
                col_all(it, tile).wait_send()


def hand_over(f, g, anc, f_out, g_out, anc_out, sems):
    copies = [
        pltpu.make_async_copy(a, b, sems.at[i]) for i, (a, b) in enumerate(((f, f_out), (g, g_out), (anc, anc_out)))
    ]
    for copy in copies:
        copy.start()
    for copy in copies:
        copy.wait()


def in_hbm_now(array):
    return pltpu.with_memory_space_constraint(array, pltpu.HBM)


def shards(sources, targets, pair_active, count_src, count_tgt):
    f32, bf16 = jnp.float32, jnp.bfloat16
    vmem, sem = pltpu.VMEM, pltpu.SemaphoreType.DMA
    in_vmem = pl.BlockSpec(memory_space=pltpu.VMEM)
    in_hbm = pl.BlockSpec(memory_space=pltpu.HBM)
    f, g, anc = pl.pallas_call(
        kernel,
        out_shape=(
            jax.ShapeDtypeStruct((1, 512), f32),
            jax.ShapeDtypeStruct((1, 4096), f32),
            jax.ShapeDtypeStruct((DIMS, LANES), f32),
        ),
        in_specs=[in_hbm] * 5,
        out_specs=(in_vmem, in_vmem, in_vmem),
        scratch_shapes=[
            pltpu.SMEM((32,), jnp.int32),
            pltpu.SMEM((8,), jnp.int32),
            pltpu.SMEM((1, 1), jnp.int32),
            vmem((4, DIMS, LANES), f32),
            vmem((X_CHIPS * CORES, 1, LANES), f32),
            vmem((2, 4, DIMS, LANES), f32),
            vmem((CORES, DIMS, COLS // 2), f32),
            vmem((PAD, ROWS), f32),
            vmem((PAD, COLS), f32),
            vmem((6 * PAD + EXTRA, COLS), bf16),
            vmem((2 * PAD, ROWS), bf16),
            vmem((COL_BLOCKS, 1, LANES), f32),
            vmem((ROWS, COLS), f32),
            vmem((ROWS, LANES), f32),
            vmem((ROWS, LANES), f32),
            vmem((ROWS, LANES), f32),
            vmem((COL_BLOCKS, 8, LANES), f32),
            vmem((COL_BLOCKS, 8, LANES), f32),
            vmem((COL_BLOCKS, 8, LANES), f32),
            vmem((ITERS, PARTS, 16, PART_BLOCKS, LANES), f32),
            vmem((ITERS, CORES, Z_CHIPS, Z_CHIPS, LANES), f32),
            vmem((ITERS, CORES, 2, Z_CHIPS, LANES), f32),
            vmem((2, PARTS, PART_BLOCKS, LANES), f32),
            vmem((X_CHIPS, Z_CHIPS, LANES), f32),
            vmem((Z_CHIPS, 56, LANES), f32),
            vmem((Z_CHIPS, 56, LANES), f32),
            vmem((Z_CHIPS, 56, LANES), f32),
            vmem((Z_CHIPS, 56, LANES), f32),
            vmem((Z_CHIPS, 56, LANES), f32),
            sem((7 + Z_CHIPS,)), sem((2,)), sem(()), sem((2, 4)), sem((2,)), sem((ITERS, PARTS)), sem((ITERS, PARTS)),
            sem((ITERS, 2)), sem((ITERS, 2)), sem((ITERS, 2)), sem((ITERS, 2)), sem((2,)), sem((2,)),
            sem(()), sem((Z_CHIPS,)), sem((2,)),
        ],
        compiler_params=pltpu.CompilerParams(
            collective_id=0, has_side_effects=True, vmem_limit_bytes=40 * 2**20
        ),
    )(in_hbm_now(count_src), in_hbm_now(count_tgt), pair_active, in_hbm_now(sources), in_hbm_now(targets))
    f, g, anc = pl.pallas_call(
        hand_over,
        out_shape=(
            jax.ShapeDtypeStruct((1, 512), f32),
            jax.ShapeDtypeStruct((1, 4096), f32),
            jax.ShapeDtypeStruct((DIMS, LANES), f32),
        ),
        in_specs=[pl.BlockSpec(memory_space=pl.ANY)] * 3,
        out_specs=(in_hbm,) * 3,
        scratch_shapes=[sem((3,))],
        compiler_params=pltpu.CompilerParams(vmem_limit_bytes=40 * 2**20),
    )(f, g, anc)
    return f.reshape(512), g.reshape(4096), anc


def solution(mesh):
    return jax.shard_map(
        shards,
        mesh=mesh,
        in_specs=(P(None, "src"), P(None, "tgt"), P("src", "tgt"), P(), P()),
        out_specs=(P("src"), P("tgt"), P(None, ("tgt", "src"))),
        check_vma=False,
    )
```

time: 83.6 us -> 79.5 us (0.951)
  local copies, waits for them, and re-layouts: 3.87 us -> 0 us
    unnamed x11 -> x0, local copies, waits for them, and re-layouts: 3.87 us -> none
where the time goes in v3:
time: 79.5 us; the launch traced here: 79.3 us
  Pallas kernels  78 us (98%)
  between operations  1.29 us (2%)
    pallas_call x1, Pallas kernels, shards(): pl.pallas_call(kernel, out_shape=(jax.ShapeDtypeStruct((1, 512), f32), ja...  77.4 us

profile of v3, /device:TPU:1, one launch (start us, length us, event | category | flops | bytes accessed | tf_op | source)
XLA Modules:
  0.0 79.3 jit_solution(15056678864833285734)
XLA Ops:
  1.3 77.4 %shard_map.76 = (f32[1,512]{1,0:T(1,128)S(1)}, f32[1,4096]{1,0:T(1,128)S(1)}, f32[50,128]{1,0:T(8,128)S(1)}) custom-call(s32[32]{0:T(128)} %counts_src.1, s32[8]{0:T(128)} %counts_tgt.1, s32[1,1]{1,0:T(1,128)S(6)} %copy.8.pairs, f32[50,512]{1,0:T(8,128)} %src.1, f32[50,4096]{1,0:T(8,128)} %tgt.1), custom_call_target="tpu_custom_call" | custom-call | tf_op jit(solution)/shard_map/pallas_call | solution.py:493
  78.7 0.6 shard_map.77

commit v4 on v3

--- a/solution.py
+++ b/solution.py
@@ -66,8 +66,8 @@
     f_out, g_out, anc_out,
     count_src, count_tgt, pair, x_own, flags, x_in, y_in, x_full, y_full, y_stack, x_pieces, y_norms,
     logits, row_peak, row_total, f_rep, g_rep, col_peak, col_total,
-    row_box, col_box, core_box, f_box, g_box, num_own, num_give, num_got, num_send, num_in,
-    own_sems, flag_sems, x_send, x_recv, y_sems, row_send, row_recv, col_send, col_recv, core_send, core_recv, f_sems, g_sems,
+    row_box, col_box, core_box, g_sum_box, f_box, g_box, num_own, num_give, num_got, num_send, num_in,
+    own_sems, flag_sems, x_send, x_recv, y_sems, row_send, row_recv, col_send, col_recv, core_send, core_recv, g_sum_sems, f_sems, g_sems,
     give_send, give_recv, num_sems,
 ):
     at_src = lax.axis_index("src")
@@ -143,7 +143,7 @@
         return total.astype(jnp.float32)
 
     log_a = -jnp.log2(jnp.full((PART_BLOCKS, LANES), number_of(count_src, Z_CHIPS * X_CHIPS), jnp.float32))
-    log_b = -jnp.log2(jnp.full((Z_CHIPS, LANES), number_of(count_tgt, Y_CHIPS * CORES), jnp.float32))
+    log_b = -jnp.log2(jnp.full((COL_BLOCKS, LANES), number_of(count_tgt, Y_CHIPS * CORES), jnp.float32))
     col_counts = [count_tgt[y * CORES + i] for i in range(CORES)]
 
     def places(shape):
@@ -156,7 +156,9 @@
 
     block, lane = places((Z_CHIPS, LANES))
     col_within = (block * X_CHIPS + x) * LANES + lane
-    col_live = [col_within < count for count in col_counts]
+    two_within = jnp.concatenate([col_within] * CORES, axis=0)
+    two_block = lax.broadcasted_iota(jnp.int32, (COL_BLOCKS, LANES), 0)
+    col_live = two_within < jnp.where(two_block < Z_CHIPS, col_counts[0], col_counts[1])
 
     x_full[DIMS:PAD, :] = jnp.zeros((PAD - DIMS, ROWS), jnp.float32)
     y_full[DIMS:PAD, :] = jnp.zeros((PAD - DIMS, COLS), jnp.float32)
@@ -276,38 +278,36 @@
         col_peak[...] = jnp.full((COL_BLOCKS, 8, LANES), LOW, jnp.float32)
         col_total[...] = jnp.zeros((COL_BLOCKS, 8, LANES), jnp.float32)
 
-    def col_sum(tile):
-        peaks = col_peak[tile * 8 : tile * 8 + 8]
+    def col_total_of():
+        peaks = col_peak[...]
         peak = jnp.max(peaks, axis=1, keepdims=True)
-        total = jnp.sum(col_total[tile * 8 : tile * 8 + 8] * jnp.exp2(peaks - peak), axis=1)
+        total = jnp.sum(col_total[...] * jnp.exp2(peaks - peak), axis=1)
         return peak[:, 0, :] + jnp.log2(total)
 
-    def col_give(it, tile, value):
-        own = col_box.at[it, tile, len(OVER_Z)]
+    def over_z(box, send, recv):
+        some = box.at[pl.ds(0, len(OVER_Z))]
+        return remote(some, some, send, recv, OVER_Z[0])
+
+    def give_over_z(box, send, recv, value):
+        own = box.at[len(OVER_Z)]
         own[...] = value
         for r, d in enumerate(OVER_Z):
-            remote(own, col_box.at[it, tile, r], col_send.at[it, tile], col_recv.at[it, tile], d).start()
-
-    def col_all(it, tile):
-        some = col_box.at[it, tile, pl.ds(0, len(OVER_Z))]
-        return remote(some, some, col_send.at[it, tile], col_recv.at[it, tile], OVER_Z[0])
-
-    def over_z(it, tile):
-        col_all(it, tile).wait_recv()
-        return log_sum([col_box[it, tile, r] for r in range(len(OVER_Z) + 1)])
-
-    def core_copy(it, tile):
-        return remote(
-            core_box.at[it, tile, 1], core_box.at[it, tile, 0], core_send.at[it, tile], core_recv.at[it, tile], OTHER_CORE
-        )
-
-    def core_give(it, tile, value):
-        core_box[it, tile, 1] = value
-        core_copy(it, tile).start()
-
-    def over_cores(it, tile):
-        core_copy(it, tile).wait_recv()
-        return log_sum([core_box[it, tile, r] for r in range(2)])
+            remote(own, box.at[r], send, recv, d).start()
+
+    def sum_over_z(box, send, recv):
+        over_z(box, send, recv).wait_recv()
+        return log_sum([box[r] for r in range(len(OVER_Z) + 1)])
+
+    def core_copy(it):
+        return remote(core_box.at[it, 1], core_box.at[it, 0], core_send.at[it], core_recv.at[it], OTHER_CORE)
+
+    def core_give(it, value):
+        core_box[it, 1] = value
+        core_copy(it).start()
+
+    def sum_over_cores(it):
+        core_copy(it).wait_recv()
+        return log_sum([core_box[it, r] for r in range(2)])
 
     for i in range(2):
         h = (x & 1) ^ jnp.where(half == c, i, 1 - i)
@@ -330,40 +330,34 @@
         lax.fori_loop(0, 4, rows_and_sums, 0)
         row_start(0, h)
 
-    def columns_from_rows(it, give):
+    def columns_from_rows(it):
         col_reset()
         for q in range(PARTS):
             f_box[0, q] = row_end(it, q)
-            if q < PARTS - 1:
-                col_sums(q, (0, 1))
-        for tile in range(CORES):
-            col_sums(PARTS - 1, (tile,))
-            give(it, tile, col_sum(tile))
+            col_sums(q, (0, 1))
+        return col_total_of()
 
     def iteration(it, _):
-        columns_from_rows(it, col_give)
-        for tile in range(CORES):
-            core_give(it, tile, over_z(it, tile))
-        for tile in range(CORES):
-            g = jnp.where(col_live[tile], log_b - over_cores(it, tile), 0.0)
-            for b in range(Z_CHIPS):
-                g_rep[tile * Z_CHIPS + b] = jnp.broadcast_to(g[b : b + 1, :], (8, LANES))
-            for q in range(PARTS):
+        mine = columns_from_rows(it)
+        give_over_z(col_box.at[it], col_send.at[it], col_recv.at[it], mine)
+        core_give(it, sum_over_z(col_box.at[it], col_send.at[it], col_recv.at[it]))
+        g = jnp.where(col_live, log_b - sum_over_cores(it), 0.0)
+        for b in range(COL_BLOCKS):
+            g_rep[b] = jnp.broadcast_to(g[b : b + 1, :], (8, LANES))
+        for q in range(PARTS):
+            for tile in range(CORES):
                 row_sums(q, tile)
-                if tile == CORES - 1:
-                    row_start(it + 1, q)
+            row_start(it + 1, q)
         return 0
 
     last = ITERS - 1
     lax.fori_loop(0, last, iteration, 0)
-    columns_from_rows(last, core_give)
+    local_sums = columns_from_rows(last)
+    core_give(last, local_sums)
     f_copy = remote(f_box.at[0], f_box.at[1], f_sems.at[0], f_sems.at[1], OTHER_CORE)
     f_copy.start()
-    both = [over_cores(last, tile) for tile in range(CORES)]
-    col_give(last, 0, jnp.where(c == 0, both[0], both[1]))
-    for tile in range(CORES):
-        for b in range(Z_CHIPS):
-            col_peak[tile * Z_CHIPS + b] = jnp.broadcast_to(both[tile][b : b + 1, :], (8, LANES))
+    for b in range(COL_BLOCKS):
+        col_peak[b] = jnp.broadcast_to(local_sums[b : b + 1, :], (8, LANES))
 
     def distance(k):
         step = (k + 1) // 2
@@ -391,15 +385,25 @@
             tiles = [acc[0:56, i * LANES : (i + 1) * LANES] for i in range(CORES)]
             num_own[k] = jnp.where(c == 0, tiles[0], tiles[1])
             num_give[k] = jnp.where(c == 0, tiles[1], tiles[0])
+            sums = [value[0:1, :] for value in local]
+            num_own[k, DIMS : DIMS + 1, :] = jnp.where(c == 0, sums[0], sums[1])
+            num_give[k, DIMS : DIMS + 1, :] = jnp.where(c == 0, sums[1], sums[0])
             give(k).start()
+
+        @pl.when(k == 2)
+        def _():
+            both = sum_over_cores(last)
+            give_over_z(g_sum_box, g_sum_sems.at[0], g_sum_sems.at[1], jnp.where(c == 0, both[0:Z_CHIPS], both[Z_CHIPS:]))
 
         @pl.when(k >= 2)
         def _():
             j = k - 2
             dz = distance(j)
             give(j).wait_recv()
-            num_send[j] = num_own[j] + num_got[j]
-            num_send[j, DIMS : DIMS + 1, :] = col_peak[c * Z_CHIPS + lax.rem(z + dz, Z_CHIPS)][0:1, :]
+            sums = [box[j, DIMS : DIMS + 1, :] for box in (num_own, num_got)]
+            both = log_sum(sums)
+            num_send[j] = num_own[j] * jnp.exp2(sums[0] - both) + num_got[j] * jnp.exp2(sums[1] - both)
+            num_send[j, DIMS : DIMS + 1, :] = both
 
             @pl.when(j < Z_CHIPS - 1)
             def _():
@@ -410,7 +414,8 @@
     lax.fori_loop(0, Z_CHIPS + 2, ancestors_of, 0)
 
     live_here = col_within < count_tgt[at_tgt]
-    g_here = jnp.where(live_here, (log_b - over_z(last, 0)) * (1.0 / SCALE), 0.0)
+    g_here = log_b[0:Z_CHIPS] - sum_over_z(g_sum_box, g_sum_sems.at[0], g_sum_sems.at[1])
+    g_here = jnp.where(live_here, g_here * (1.0 / SCALE), 0.0)
     for k in range(Z_CHIPS):
         norm = y_norms[c * Z_CHIPS + k]
         within = (k * X_CHIPS + x) * LANES + lax.broadcasted_iota(jnp.int32, (1, LANES), 1)
@@ -464,11 +469,11 @@
         return 0
 
     lax.fori_loop(0, ITERS, sent, 0)
+    over_z(g_sum_box, g_sum_sems.at[0], g_sum_sems.at[1]).wait_send()
     for it in range(ITERS):
-        for tile in range(CORES):
-            core_copy(it, tile).wait_send()
-            if it < last or tile == 0:
-                col_all(it, tile).wait_send()
+        core_copy(it).wait_send()
+        if it < last:
+            over_z(col_box.at[it], col_send.at[it], col_recv.at[it]).wait_send()
 
 
 def hand_over(f, g, anc, f_out, g_out, anc_out, sems):
@@ -520,8 +525,9 @@
             vmem((COL_BLOCKS, 8, LANES), f32),
             vmem((COL_BLOCKS, 8, LANES), f32),
             vmem((ITERS, PARTS, 16, PART_BLOCKS, LANES), f32),
-            vmem((ITERS, CORES, Z_CHIPS, Z_CHIPS, LANES), f32),
-            vmem((ITERS, CORES, 2, Z_CHIPS, LANES), f32),
+            vmem((ITERS, Z_CHIPS, COL_BLOCKS, LANES), f32),
+            vmem((ITERS, 2, COL_BLOCKS, LANES), f32),
+            vmem((Z_CHIPS, Z_CHIPS, LANES), f32),
             vmem((2, PARTS, PART_BLOCKS, LANES), f32),
             vmem((X_CHIPS, Z_CHIPS, LANES), f32),
             vmem((Z_CHIPS, 56, LANES), f32),
@@ -530,7 +536,7 @@
             vmem((Z_CHIPS, 56, LANES), f32),
             vmem((Z_CHIPS, 56, LANES), f32),
             sem((7 + Z_CHIPS,)), sem((2,)), sem(()), sem((2, 4)), sem((2,)), sem((ITERS, PARTS)), sem((ITERS, PARTS)),
-            sem((ITERS, 2)), sem((ITERS, 2)), sem((ITERS, 2)), sem((ITERS, 2)), sem((2,)), sem((2,)),
+            sem((ITERS,)), sem((ITERS,)), sem((ITERS,)), sem((ITERS,)), sem((2,)), sem((2,)), sem((2,)),
             sem(()), sem((Z_CHIPS,)), sem((2,)),
         ],
         compiler_params=pltpu.CompilerParams(

time: 79.5 us -> 78.4 us (0.986)
  Pallas kernels: 78 us -> 76.9 us
    pallas_call x1, Pallas kernels: 77.4 us -> 76.2 us  [shards(): pl.pallas_call(kernel, out_shape=(jax.ShapeDtypeStruct((1, 512), f32), ja...]
where the time goes in v4:
time: 78.4 us; the launch traced here: 78.2 us
  Pallas kernels  76.9 us (98%)
  between operations  1.29 us (2%)
    pallas_call x1, Pallas kernels, shards(): pl.pallas_call(kernel, out_shape=(jax.ShapeDtypeStruct((1, 512), f32), ja...  76.2 us

profile of v4, /device:TPU:1, one launch (start us, length us, event | category | flops | bytes accessed | tf_op | source)
XLA Modules:
  0.0 78.2 jit_solution(693397808500650704)
XLA Ops:
  1.3 76.2 %shard_map.76 = (f32[1,512]{1,0:T(1,128)S(1)}, f32[1,4096]{1,0:T(1,128)S(1)}, f32[50,128]{1,0:T(8,128)S(1)}) custom-call(s32[32]{0:T(128)} %counts_src.1, s32[8]{0:T(128)} %counts_tgt.1, s32[1,1]{1,0:T(1,128)S(6)} %copy.8.pairs, f32[50,512]{1,0:T(8,128)} %src.1, f32[50,4096]{1,0:T(8,128)} %tgt.1), custom_call_target="tpu_custom_call" | custom-call | tf_op jit(solution)/shard_map/pallas_call | solution.py:498
  77.5 0.6 shard_map.77

commit v5 on v4

--- a/solution.py
+++ b/solution.py
@@ -113,26 +113,27 @@
     ]
     for copy in scalars:
         copy.start()
+    pl.semaphore_wait(barrier, len(PARTNERS))
+
+    x_copies = [
+        remote(src.at[:, lanes(k)], x_in.at[x & 1, k], x_send, x_recv.at[x & 1, k], d) for k in range(4) for d in OVER_X
+    ]
+
+    @pl.when(half == c)
+    def _():
+        for copy in x_copies:
+            copy.start()
+
+    for k in range(Z_CHIPS):
+        whole = tgt.at[:, lanes(k * X_CHIPS + x)]
+        remote(whole, y_in.at[c, :, lanes(k)], y_sems.at[0], y_sems.at[1], OTHER_CORE).start()
+    y_copy = remote(y_in.at[1 - c], y_in.at[1 - c], y_sems.at[0], y_sems.at[1], OTHER_CORE)
+
     for copy in scalars:
         copy.wait()
     mine = x * CORES + c
     listed = (pair[0, 0] > 0).astype(jnp.float32)
     flags[mine] = jnp.full((1, LANES), listed, jnp.float32)
-    for copy in x_local + y_local:
-        copy.wait()
-    pl.semaphore_wait(barrier, len(PARTNERS))
-
-    x_copies = [
-        remote(x_own.at[k], x_in.at[x & 1, k], x_send, x_recv.at[x & 1, k], d) for k in range(4) for d in OVER_X
-    ]
-
-    @pl.when(half == c)
-    def _():
-        for copy in x_copies:
-            copy.start()
-
-    y_copy = remote(y_in.at[c], y_in.at[c], y_sems.at[0], y_sems.at[1], OTHER_CORE)
-    y_copy.start()
     for d in OVER_X_CORE:
         remote(flags.at[mine], flags.at[mine], flag_sems.at[0], flag_sems.at[1], d).start()
 
@@ -179,6 +180,8 @@
 
         lax.fori_loop(0, Z_CHIPS, body, 0)
 
+    for copy in x_local + y_local:
+        copy.wait()
     columns_of(c)
     y_copy.wait_recv()
     columns_of(1 - c)
@@ -193,48 +196,60 @@
         extra = jnp.where(line == 0, rows[0], jnp.where(line == 1, rows[1], jnp.where(line == 2, 1.0, 0.0)))
         y_stack[6 * PAD :, b * LANES : (b + 1) * LANES] = extra.astype(jnp.bfloat16)
 
-    def rows_of(h, k):
+    def rows_of(h, pair):
         live = count_src[z * X_CHIPS + 2 * c + h]
-        at = lanes(4 * h + k)
-        x_full[0:DIMS, at] = x_in[h, k]
-        whole = x_full[:, at]
-        q1, q2 = split(whole, 2)
-        x_pieces[0:PAD, at] = q1
-        x_pieces[PAD:, at] = q2
-        p1, p2, p3 = split(whole * (2.0 * SCALE), 3)
-        dead = jnp.where(k * LANES + lane < live, 0.0, NEG)
-        extra = jnp.where(line == 2, dead, jnp.where(line == h, 1.0, 0.0))
-        stack = jnp.concatenate([p1, p1, p2, p1, p3, p2, extra.astype(jnp.bfloat16)], axis=0)
-        rows = stack.T
+        lines = []
+        for i in range(2):
+            k = 2 * pair + i
+            at = lanes(4 * h + k)
+            x_full[0:DIMS, at] = x_in[h, k]
+            p1, p2, p3 = split(x_full[:, at] * (2.0 * SCALE), 3)
+            dead = jnp.where(k * LANES + lane < live, 0.0, NEG)
+            extra = jnp.where(line == 2, dead, jnp.where(line == h, 1.0, 0.0))
+            lines.append(jnp.concatenate([p1, p1, p2, p1, p3, p2, extra.astype(jnp.bfloat16)], axis=0).T)
+        rows = jnp.concatenate(lines, axis=0)
+        at = lanes(2 * h + pair, 2 * LANES)
+        here, peaks, totals = logits.at[at], row_peak.at[at], row_total.at[at]
         for i in range(COLS // 256):
             cols = slice(i * 256, (i + 1) * 256)
-            logits[at, cols] = jnp.dot(rows, y_stack[:, cols], preferred_element_type=jnp.float32)
+            here[:, cols] = jnp.dot(rows, y_stack[:, cols], preferred_element_type=jnp.float32)
+            if i == 3:
+                row_sums_in(here, peaks, totals, 0)
+        row_sums_in(here, peaks, totals, 1)
+
+    def pieces_of(k, _):
+        first, second = split(x_full[:, lanes(k)], 2)
+        x_pieces[0:PAD, lanes(k)] = first
+        x_pieces[PAD:, lanes(k)] = second
+        return 0
 
     def row_all(it, q):
         some = row_box.at[it, q, pl.ds(0, len(OVER_XY))]
         return remote(some, some, row_send.at[it, q], row_recv.at[it, q], OVER_XY[0])
 
-    def row_sums_at(base, tile):
+    def row_sums_in(here, peaks, totals, tile):
         g = [g_rep[tile * 8 + b] for b in range(8)]
-        for i in range(16):
-            at = pl.ds(pl.multiple_of(base + 8 * i, 8), 8)
-            parts = [logits[at, (tile * 8 + b) * LANES : (tile * 8 + b + 1) * LANES] + g[b] for b in range(8)]
+        for i in range(here.shape[0] // 8):
+            at = slice(8 * i, 8 * i + 8)
+            parts = [here[at, (tile * 8 + b) * LANES : (tile * 8 + b + 1) * LANES] + g[b] for b in range(8)]
             best = tree(jnp.maximum, parts)
             if tile:
-                peak = row_peak[at, :]
+                peak = peaks[at, :]
                 best = jnp.maximum(best, peak)
             total = tree(jnp.add, [jnp.exp2(p - best) for p in parts])
             if tile:
-                total += row_total[at, :] * jnp.exp2(peak - best)
-            row_peak[at, :] = best
-            row_total[at, :] = total
-
-    def row_sums(q, tile):
+                total += totals[at, :] * jnp.exp2(peak - best)
+            peaks[at, :] = best
+            totals[at, :] = total
+
+    def row_sums(q):
         def body(k, _):
-            row_sums_at(q * PART_ROWS + k * LANES, tile)
+            at = lanes(q * PART_BLOCKS + k)
+            for tile in range(CORES):
+                row_sums_in(logits.at[at], row_peak.at[at], row_total.at[at], tile)
             return 0
 
-        lax.fori_loop(0, PART_BLOCKS, body, 0)
+        lax.fori_loop(0, PART_BLOCKS, body, 0, unroll=2)
 
     def row_start(it, q):
         own = row_box.at[it, q, len(OVER_XY)]
@@ -317,18 +332,20 @@
         def _():
             x_in[h] = x_own[...]
 
-        def rows_and_sums(k, _):
+        def rows_and_sums(pair, _):
             @pl.when(jnp.logical_not(here))
             def _():
-                remote(x_in.at[h, k], x_in.at[h, k], x_send, x_recv.at[h, k], OVER_X[0]).wait_recv()
-
-            rows_of(h, k)
-            for tile in range(CORES):
-                row_sums_at((4 * h + k) * LANES, tile)
+                for i in range(2):
+                    k = 2 * pair + i
+                    remote(x_in.at[h, k], x_in.at[h, k], x_send, x_recv.at[h, k], OVER_X[0]).wait_recv()
+
+            rows_of(h, pair)
             return 0
 
-        lax.fori_loop(0, 4, rows_and_sums, 0)
+        lax.fori_loop(0, 2, rows_and_sums, 0)
         row_start(0, h)
+
+    lax.fori_loop(0, 2 * 4, pieces_of, 0)
 
     def columns_from_rows(it):
         col_reset()
@@ -345,8 +362,7 @@
         for b in range(COL_BLOCKS):
             g_rep[b] = jnp.broadcast_to(g[b : b + 1, :], (8, LANES))
         for q in range(PARTS):
-            for tile in range(CORES):
-                row_sums(q, tile)
+            row_sums(q)
             row_start(it + 1, q)
         return 0
 
@@ -382,7 +398,7 @@
                 w1, w2 = split(weight, 2)
                 two = jnp.dot(x_pieces[:, at], w1, preferred_element_type=jnp.float32)
                 acc += two[0:PAD] + two[PAD:] + jnp.dot(x_pieces[0:PAD, at], w2, preferred_element_type=jnp.float32)
-            tiles = [acc[0:56, i * LANES : (i + 1) * LANES] for i in range(CORES)]
+            tiles = [acc[0 : DIMS + 1, i * LANES : (i + 1) * LANES] for i in range(CORES)]
             num_own[k] = jnp.where(c == 0, tiles[0], tiles[1])
             num_give[k] = jnp.where(c == 0, tiles[1], tiles[0])
             sums = [value[0:1, :] for value in local]
@@ -530,11 +546,11 @@
             vmem((Z_CHIPS, Z_CHIPS, LANES), f32),
             vmem((2, PARTS, PART_BLOCKS, LANES), f32),
             vmem((X_CHIPS, Z_CHIPS, LANES), f32),
-            vmem((Z_CHIPS, 56, LANES), f32),
-            vmem((Z_CHIPS, 56, LANES), f32),
-            vmem((Z_CHIPS, 56, LANES), f32),
-            vmem((Z_CHIPS, 56, LANES), f32),
-            vmem((Z_CHIPS, 56, LANES), f32),
+            vmem((Z_CHIPS, DIMS + 1, LANES), f32),
+            vmem((Z_CHIPS, DIMS + 1, LANES), f32),
+            vmem((Z_CHIPS, DIMS + 1, LANES), f32),
+            vmem((Z_CHIPS, DIMS + 1, LANES), f32),
+            vmem((Z_CHIPS, DIMS + 1, LANES), f32),
             sem((7 + Z_CHIPS,)), sem((2,)), sem(()), sem((2, 4)), sem((2,)), sem((ITERS, PARTS)), sem((ITERS, PARTS)),
             sem((ITERS,)), sem((ITERS,)), sem((ITERS,)), sem((ITERS,)), sem((2,)), sem((2,)), sem((2,)),
             sem(()), sem((Z_CHIPS,)), sem((2,)),

time: 78.4 us -> 76.3 us (0.973)
  Pallas kernels: 76.9 us -> 74.9 us
    pallas_call x1, Pallas kernels: 76.2 us -> 74.3 us  [shards(): pl.pallas_call(kernel, out_shape=(jax.ShapeDtypeStruct((1, 512), f32), ja...]
where the time goes in v5:
time: 76.3 us; the launch traced here: 76.2 us
  Pallas kernels  74.9 us (98%)
  between operations  1.29 us (2%)
    pallas_call x1, Pallas kernels, shards(): pl.pallas_call(kernel, out_shape=(jax.ShapeDtypeStruct((1, 512), f32), ja...  74.3 us

profile of v5, /device:TPU:1, one launch (start us, length us, event | category | flops | bytes accessed | tf_op | source)
XLA Modules:
  0.0 76.2 jit_solution(9274682809804154983)
XLA Ops:
  1.3 74.3 %shard_map.76 = (f32[1,512]{1,0:T(1,128)S(1)}, f32[1,4096]{1,0:T(1,128)S(1)}, f32[50,128]{1,0:T(8,128)S(1)}) custom-call(s32[32]{0:T(128)} %counts_src.1, s32[8]{0:T(128)} %counts_tgt.1, s32[1,1]{1,0:T(1,128)S(6)} %copy.8.pairs, f32[50,512]{1,0:T(8,128)} %src.1, f32[50,4096]{1,0:T(8,128)} %tgt.1), custom_call_target="tpu_custom_call" | custom-call | tf_op jit(solution)/shard_map/pallas_call | solution.py:514
  75.6 0.6 shard_map.77
